TPU v7x, 32 devices: a whole 2x2x4 slice. The times are simulated.
32 devices in a mesh: grp: 2 (over y), ctx: 4 (over z), head: 2 (over x), sub: 2 (over core).
Axes of the slice: x: 2, y: 2, z: 4, core: 2. Of those that a mesh axis runs over, the one named last changes fastest.
Arguments:
- queries: bfloat16 [512, 16384], P(('grp', 'ctx', 'head', 'sub')), parts along dimension 0, may hold values from -400 to 400
- kv_cache: bfloat16 [2, 8192, 1024], P(None, ('grp', 'ctx', 'sub'), 'head'), parts along dimension 1, may hold values from -6 to 6
- page_counts: int32 [8], P('grp'), parts along dimension 0, may hold values from 1 to 4, as said below
Outputs:
- attended: bfloat16 [512, 16384], P(('grp', 'ctx', 'head', 'sub')), parts along dimension 0
There are 2 independent parts, one for each index of `grp`. A program takes and returns all parts, laid end to end along the dimension named above; each array names one. Nothing has to cross between parts.
Inputs may be any that keep to these rules, and one draw needn't show every extreme that they name: `page_counts`: each count is at least 1, the counts sum to exactly 8, and one request has exactly 4 pages.
All inputs are finite; a program needn't handle non-finite values.
Results may differ from a plain program's by a relative error of at most 0.014.
Values may be sent and summed in bfloat16 or wider, within the bound.
No kernel may reach another device: no remote copies, remote signals or barrier semaphores. Data moves between devices by JAX's collectives and lax.ppermute only.
A program may use at most 64 MiB of HBM per device.

v0:
```python
import functools

import jax
import jax.numpy as jnp
from jax import lax
from jax.experimental import pallas as pl
from jax.experimental.pallas import tpu as pltpu
from jax.sharding import PartitionSpec as P

HQ = 128
KVH = 8
HD = 128
REQS = 4
QR = 64
PAGE = 256
SPAN = 256


NEG = -1e30
EXP2_SCALE = HD ** (-0.5) * 1.4426950408889634


def run(copies):
    for copy in copies:
        copy.start()
    for copy in copies:
        copy.wait()


def head_part(step, width):
    return pl.ds(pl.multiple_of((lax.axis_index("head") ^ step) * width, width), width)


def split_kernel(queries, *refs):
    outs, sems = refs[:-1], refs[-1]
    run([
        pltpu.make_async_copy(queries.at[:, head_part(step, out.shape[1])], out, sems.at[step])
        for step, out in enumerate(outs)
    ])


def join_kernel(keys, *refs):
    out, sems = refs[-2:]
    for i, (step, source) in enumerate(keys):
        @pl.when(lax.axis_index("sub") == source)
        def _():
            run([pltpu.make_async_copy(refs[i], out.at[:, head_part(step, refs[i].shape[1])], sems.at[0])])


def own_pair_of(low_ctx, sub_count):
    return (lax.axis_index("ctx") - low_ctx) * sub_count + lax.axis_index("sub")


def gather_kernel(low_ctx, sub_count, counts, own, far, paired, after, out):
    local_kv, most_pages = out.shape[:2]
    own_pair = own_pair_of(low_ctx, sub_count)
    sub = lax.axis_index("sub")

    @pl.when(lax.axis_index("ctx") >= low_ctx)
    def _():
        start = jnp.int32(0)
        for r in range(REQS):
            start = start + jnp.where(r < own_pair, counts[r], 0)
        count = counts[own_pair]
        for p in range(most_pages):
            page = start + p
            apart = page // 2 - own_pair
            which = jnp.where(apart == 0, 0, jnp.where(apart == 1 - 2 * sub, 1, 2))
            page_rows = pl.ds(pl.multiple_of(lax.rem(page, 2) * PAGE, PAGE), PAGE)
            for n, ref in enumerate((own, paired, far)):
                @pl.when((p < count) & (which == n))
                def _():
                    for g in range(local_kv):
                        for i in range(2):
                            out[g, p, i] = ref[i, page_rows, g * HD:(g + 1) * HD]


def attend_kernel(low_ctx, sub_count, step, source_sub, waits, counts, pages_in, queries, *refs):
    out = refs[waits]
    head = lax.axis_index("head")
    tokens, width = queries.shape
    local_kv, most_pages = pages_in.shape[:2]
    span = width // local_kv
    per_group = span // HD
    rows = per_group * tokens
    first_token = ((head ^ step) * sub_count + source_sub) * tokens

    def attend(pages):
        token = lax.rem(lax.broadcasted_iota(jnp.int32, (rows, PAGE), 0), tokens)
        column = lax.broadcasted_iota(jnp.int32, (rows, PAGE), 1)
        visible = column <= PAGE - QR + first_token + token

        def scores_of(g):
            q_block = queries[:, g * span:(g + 1) * span]
            q_rows = jnp.concatenate([q_block[:, j * HD:(j + 1) * HD] for j in range(per_group)], axis=0)
            for p in range(pages):
                scores = lax.dot_general(
                    q_rows, pages_in[g, p, 0], (((1,), (1,)), ((), ())), preferred_element_type=jnp.float32
                )
                yield jnp.where(visible, scores, NEG) if p == pages - 1 else scores

        scores = list(scores_of(0))
        for g in range(local_kv):
            following = scores_of(g + 1) if g + 1 < local_kv else iter(())
            later = []
            top = jnp.max(functools.reduce(jnp.maximum, scores), axis=1, keepdims=True)
            totals, product = None, None
            for p in range(pages):
                later += [s for _, s in zip(range(1), following)]
                numerators = jnp.exp2((scores[p] - top) * EXP2_SCALE)
                part = jnp.dot(
                    numerators.astype(jnp.bfloat16), pages_in[g, p, 1], preferred_element_type=jnp.float32
                )
                totals = numerators if p == 0 else totals + numerators
                product = part if p == 0 else product + part
            totals = jnp.sum(totals, axis=1, keepdims=True)
            done = (product / totals).astype(jnp.bfloat16)
            out[:, g * span:(g + 1) * span] = jnp.concatenate(
                [done[j * tokens:(j + 1) * tokens] for j in range(per_group)], axis=1
            )
            scores = later

    @pl.when(lax.axis_index("ctx") >= low_ctx)
    def _():
        count = counts[own_pair_of(low_ctx, sub_count)]
        for pages in [*range(1, most_pages - REQS + 3), most_pages]:
            @pl.when(count == pages)
            def _():
                attend(pages)


def one_request_each(queries, kv_cache, page_counts):
    ctx_size, sub_size = lax.axis_size("ctx"), lax.axis_size("sub")
    head_count = lax.axis_size("head")
    low_ctx = ctx_size // 2
    most_pages = kv_cache.shape[1] // PAGE * ctx_size * sub_size // 4
    local_kv = kv_cache.shape[2] // HD
    tokens, width = queries.shape[0], queries.shape[1] // head_count
    anywhere = pl.BlockSpec(memory_space=pl.ANY)
    in_vmem = pl.BlockSpec(memory_space=pltpu.VMEM)
    q_piece = pltpu.VMEM((tokens, width), queries.dtype)

    def vmem(array):
        return pltpu.with_memory_space_constraint(array, pltpu.VMEM)

    def hbm(array):
        return pltpu.with_memory_space_constraint(array, pltpu.HBM)

    def moved(array, routes):
        def flat(place):
            return (place[0] * head_count + place[1]) * sub_size + place[2]

        return lax.ppermute(array, ("ctx", "head", "sub"), [(flat(a), flat(b)) for a, b in routes])

    def worker(request, head):
        return low_ctx + request // sub_size, head, request % sub_size

    heads = range(head_count)
    q_out = pl.pallas_call(
        split_kernel,
        out_shape=[q_piece] * head_count,
        in_specs=[anywhere],
        out_specs=[anywhere] * head_count,
        scratch_shapes=[pltpu.SemaphoreType.DMA((head_count,))],
        compiler_params=pltpu.CompilerParams(vmem_limit_bytes=2**20),
        name="split",
    )(hbm(queries))
    routes = {
        (step, s): [((r, h, s), worker(r, h ^ step)) for r in range(ctx_size) for h in heads]
        for step in heads[::-1] for s in range(sub_size)
    }
    q_in = {key: moved(q_out[key[0]], pairs) for key, pairs in routes.items()}
    first = list(routes)[0]

    middle = [(low_ctx, sub_size - 1), (low_ctx + 1, 0)]
    far = moved(kv_cache, [((a[0], h, a[1]), (b[0], h, b[1])) for a, b in (middle, middle[::-1]) for h in heads])
    paired = moved(
        kv_cache, [((c, h, s), (c, h, 1 - s)) for c in range(low_ctx, ctx_size) for h in heads for s in range(sub_size)]
    )
    first_here = pl.pallas_call(
        lambda *refs: None,
        out_shape=pltpu.VMEM((8, HD), jnp.float32),
        in_specs=[anywhere] * 2,
        out_specs=anywhere,
        cost_estimate=pl.CostEstimate(flops=2 * 10**10, bytes_accessed=2**20, transcendentals=0),
        compiler_params=pltpu.CompilerParams(vmem_limit_bytes=2**20),
        name="first_here",
    )(vmem(q_in[first]), vmem(far))
    gathered = pl.pallas_call(
        functools.partial(gather_kernel, low_ctx, sub_size),
        out_shape=pltpu.VMEM((local_kv, most_pages, 2, PAGE, HD), kv_cache.dtype),
        in_specs=[pl.BlockSpec(memory_space=pltpu.SMEM)] + [in_vmem] * 3 + [anywhere],
        out_specs=in_vmem,
        compiler_params=pltpu.CompilerParams(vmem_limit_bytes=2**20),
        name="gather",
    )(page_counts, vmem(kv_cache), vmem(far), vmem(paired), vmem(first_here))

    back = {}
    after = []
    for step, s in routes:
        out = pl.pallas_call(
            functools.partial(attend_kernel, low_ctx, sub_size, step, s, len(after)),
            out_shape=q_piece,
            in_specs=[pl.BlockSpec(memory_space=pltpu.SMEM)] + [in_vmem] * 2 + [anywhere] * len(after),
            out_specs=in_vmem,
            compiler_params=pltpu.CompilerParams(vmem_limit_bytes=12 * 2**20),
            cost_estimate=pl.CostEstimate(flops=6 * 10**9, bytes_accessed=2**22, transcendentals=10**6),
            name=f"attend_{step}{s}",
        )(page_counts, vmem(gathered), vmem(q_in[step, s]), *after)
        back[step, s] = moved(out, [(b, a) for a, b in routes[step, s]])
        after = [out]

    joined = []
    for keys in [[key for key in routes if key[0]]] + [[key] for key in routes if not key[0]]:
        joined = [
            pl.pallas_call(
                functools.partial(join_kernel, keys),
                out_shape=pltpu.HBM(queries.shape, queries.dtype),
                in_specs=[anywhere] * (len(keys) + len(joined)),
                out_specs=anywhere,
                scratch_shapes=[pltpu.SemaphoreType.DMA((1,))],
                input_output_aliases={len(keys): 0} if joined else {},
                compiler_params=pltpu.CompilerParams(vmem_limit_bytes=2**20),
                name="join",
            )(*[vmem(back[key]) for key in keys], *map(hbm, joined))
        ]
    return joined[0]


def from_behind(array, axis, by):
    count = lax.axis_size(axis)
    pairs = [(i, i + by) for i in range(count) if 0 <= i + by < count]
    return lax.ppermute(array, axis, pairs)


def queries_to_pages(queries, kv_cache, page_counts):
    per_group = HQ // KVH
    local_heads = kv_cache.shape[2] // HD
    ctx_size = lax.axis_size("ctx")
    sub_size = lax.axis_size("sub")
    head_count = lax.axis_size("head")
    tok_rows = queries.shape[0]
    score_scale = HD ** (-0.5)
    regrouped = lax.all_to_all(queries, "head", split_axis=1, concat_axis=0, tiled=True)
    all_queries = lax.all_gather(regrouped, ("ctx", "sub"), axis=0, tiled=True)
    all_queries = all_queries.reshape(SPAN, local_heads, per_group, HD)
    page_ends = jnp.cumsum(page_counts)
    ctx_rows = SPAN // ctx_size
    offsets = jnp.arange(QR, dtype=jnp.int32)
    columns = jnp.arange(PAGE, dtype=jnp.int32)
    flat_index = lax.axis_index("ctx") * sub_size + lax.axis_index("sub")
    pages_here = kv_cache.shape[1] // PAGE
    base_pages = pages_here * ctx_size * sub_size // 2
    initial = (
        jnp.full((SPAN, local_heads, per_group), NEG, jnp.float32),
        jnp.zeros((SPAN, local_heads, per_group), jnp.float32),
        jnp.zeros((SPAN, local_heads, per_group, HD), jnp.float32),
    )
    half_rows = kv_cache.shape[1] // 2
    arrived = from_behind(kv_cache[:, half_rows:], "ctx", -(ctx_size // 2))
    is_lower = lax.axis_index("ctx") < ctx_size // 2
    source_flat = flat_index + ctx_size // 2 * sub_size
    working = jnp.where(is_lower, arrived, kv_cache[:, :half_rows])
    first_page = jnp.where(
        is_lower, source_flat * pages_here + pages_here // 2, flat_index * pages_here
    )
    page_total = working.shape[1] // PAGE

    def add_page(page_turn, running):
        page_index = first_page + page_turn
        relative = page_index - base_pages
        counted = jnp.sum((relative >= page_ends).astype(jnp.int32))
        request = jnp.where(relative < 0, REQS, counted)

        def update(partial_value):
            run_max, run_sum, run_out = partial_value
            request_id = jnp.minimum(request, REQS - 1)
            row_start = request_id * QR
            gathered = row_start + offsets
            within = gathered % ctx_rows
            ctx_block = gathered // ctx_rows
            sub_part = within // (head_count * tok_rows)
            head_part = within // tok_rows % head_count
            tok_part = within % tok_rows
            natural = ctx_block * ctx_rows + (head_part * sub_size + sub_part) * tok_rows + tok_part
            query_pos = (page_ends[request_id] + base_pages) * PAGE - QR + natural - row_start
            key_pos = page_index * PAGE + columns
            visible = key_pos[None, :] <= query_pos[:, None]
            page_keys = working[0].reshape(PAGE, local_heads, HD)
            page_values = working[1].reshape(PAGE, local_heads, HD)
            query_rows = lax.dynamic_slice_in_dim(all_queries, row_start, QR, 0)
            scores = (
                jnp.einsum(
                    "qkgd,pkd->qkgp", query_rows, page_keys, preferred_element_type=jnp.float32
                )
                * score_scale
            )
            scores = jnp.where(visible[:, None, None, :], scores, NEG)
            old_max = lax.dynamic_slice_in_dim(run_max, row_start, QR, 0)
            old_sum = lax.dynamic_slice_in_dim(run_sum, row_start, QR, 0)
            old_out = lax.dynamic_slice_in_dim(run_out, row_start, QR, 0)
            new_max = jnp.maximum(old_max, jnp.max(scores, axis=3))
            factor = jnp.exp(old_max - new_max)
            numerators = jnp.exp(scores - new_max[..., None])
            new_sum = old_sum * factor + jnp.sum(numerators, axis=3)
            product = jnp.einsum(
                "qkgp,pkd->qkgd",
                numerators.astype(jnp.bfloat16),
                page_values,
                preferred_element_type=jnp.float32,
            )
            new_out = old_out * factor[..., None] + product
            return (
                lax.dynamic_update_slice_in_dim(run_max, new_max, row_start, 0),
                lax.dynamic_update_slice_in_dim(run_sum, new_sum, row_start, 0),
                lax.dynamic_update_slice_in_dim(run_out, new_out, row_start, 0),
            )

        def unchanged(partial_value):
            return partial_value

        return lax.cond(request < REQS, update, unchanged, running)

    run_max, run_sum, run_out = lax.fori_loop(0, page_total, add_page, initial)
    share = SPAN // (ctx_size * sub_size)
    global_max = lax.pmax(run_max, ("ctx", "sub"))
    factor = jnp.exp(run_max - global_max)
    sums_here, outs_here = (
        lax.psum_scatter(
            (run_sum * factor).astype(jnp.bfloat16), ("ctx", "sub"), scatter_dimension=0, tiled=True
        ).astype(jnp.float32),
        lax.psum_scatter(
            (run_out * factor[..., None]).astype(jnp.bfloat16),
            ("ctx", "sub"),
            scatter_dimension=0,
            tiled=True,
        ).astype(jnp.float32),
    )
    finished = (outs_here / sums_here[..., None]).astype(jnp.bfloat16)
    finished = finished.reshape(share, local_heads * per_group * HD)
    return lax.all_to_all(finished, "head", split_axis=0, concat_axis=1, tiled=True)


def per_device(queries, kv_cache, page_counts):
    ctx_size, sub_size, head_count = lax.axis_size("ctx"), lax.axis_size("sub"), lax.axis_size("head")
    small = (
        ctx_size == REQS == 4
        and head_count == sub_size == 2
        and kv_cache.shape[1] == 2 * PAGE
        and kv_cache.shape[2] % (sub_size * HD) == 0
        and queries.shape[0] % 16 == 0
        and queries.shape[0] * head_count * sub_size == QR
    )
    return (one_request_each if small else queries_to_pages)(queries, kv_cache, page_counts)


def solution(mesh):
    return jax.shard_map(
        per_device,
        mesh=mesh,
        in_specs=(
            P(("grp", "ctx", "head", "sub"), None),
            P(None, ("grp", "ctx", "sub"), "head"),
            P("grp"),
        ),
        out_specs=P(("grp", "ctx", "head", "sub"), None),
        check_vma=False,
    )
```

profile of v0, /device:TPU:13, one launch (start us, length us, event | category | flops | bytes accessed | tf_op | source)
XLA Modules:
  0.0 47.4 jit_solution(3146285864236757257)
XLA Ops:
  0.0 0.7 %collective-permute-start = (bf16[2,512,512]{2,1,0:T(8,128)(2,1)}, bf16[2,512,512]{2,1,0:T(8,128)(2,1)S(1)}, u32[]{:S(2)}, u32[]{:S(2)}) collective-permute-start(bf16[2,512,512]{2,1,0:T(8,128)(2,1)} %own.1), channel_id=1, source_target_pairs={{9,12},{11,14},{12,9},{14,11},{25,28},{27,30},{28,25},{30,27}} | collective-permute-start | bytes 3145736 | tf_op jit(solution)/shard_map/ppermute | solution.py:153
  0.7 1.1 %split.1 = (bf16[16,8192]{1,0:T(8,128)(2,1)S(1)}, bf16[16,8192]{1,0:T(8,128)(2,1)S(1)}) custom-call(bf16[16,16384]{1,0:T(8,128)(2,1)} %queries.1), custom_call_target="tpu_custom_call" | custom-call | tf_op jit(solution)/shard_map/split/pallas_call | solution.py:159
  1.8 0.7 %collective-permute-start.2 = (bf16[16,8192]{1,0:T(8,128)(2,1)S(1)}, bf16[16,8192]{1,0:T(8,128)(2,1)S(1)}, u32[]{:S(2)}, u32[]{:S(2)}) collective-permute-start(bf16[16,8192]{1,0:T(8,128)(2,1)S(1)} %get-tuple-element.7), channel_id=1, source_target_pairs={{0,10},{2,8},{4,11},{6,9},{8,14},{10,12},{12,15},{14,13},{16,26},{... | collective-permute-start | bytes 786440 | tf_op jit(solution)/shard_map/ppermute | solution.py:153
  2.5 0.7 %collective-permute-start.1 = (bf16[2,512,512]{2,1,0:T(8,128)(2,1)}, bf16[2,512,512]{2,1,0:T(8,128)(2,1)S(1)}, u32[]{:S(2)}, u32[]{:S(2)}) collective-permute-start(bf16[2,512,512]{2,1,0:T(8,128)(2,1)} %own.1), channel_id=1, source_target_pairs={{8,9},{9,8},{10,11},{11,10},{12,13},{13,12},{14,15},{15,14},{24,25... | collective-permute-start | bytes 3145736 | tf_op jit(solution)/shard_map/ppermute | solution.py:153
  3.2 10.0 %collective-permute-start.5 = (bf16[16,8192]{1,0:T(8,128)(2,1)S(1)}, bf16[16,8192]{1,0:T(8,128)(2,1)S(1)}, u32[]{:S(2)}, u32[]{:S(2)}) collective-permute-start(bf16[16,8192]{1,0:T(8,128)(2,1)S(1)} %get-tuple-element.7), channel_id=1, source_target_pairs={{1,10},{3,8},{5,11},{7,9},{9,14},{11,12},{13,15},{15,13},{17,26},{... | collective-permute-start | bytes 786440 | tf_op jit(solution)/shard_map/ppermute | solution.py:153
  13.2 0.0 copy-start
  13.2 0.0 copy-start.1
  13.2 0.8 %collective-permute-start.4 = (bf16[16,8192]{1,0:T(8,128)(2,1)S(1)}, bf16[16,8192]{1,0:T(8,128)(2,1)S(1)}, u32[]{:S(2)}, u32[]{:S(2)}) collective-permute-start(bf16[16,8192]{1,0:T(8,128)(2,1)S(1)} %get-tuple-element.8), channel_id=1, source_target_pairs={{0,8},{2,10},{4,9},{6,11},{8,12},{10,14},{12,13},{14,15},{16,24},{... | collective-permute-start | bytes 786440 | tf_op jit(solution)/shard_map/ppermute | solution.py:153
  14.0 0.0 collective-permute-done.2.refs_0_.queries
  14.0 3.8 %collective-permute-start.3 = (bf16[16,8192]{1,0:T(8,128)(2,1)S(1)}, bf16[16,8192]{1,0:T(8,128)(2,1)S(1)}, u32[]{:S(2)}, u32[]{:S(2)}) collective-permute-start(bf16[16,8192]{1,0:T(8,128)(2,1)S(1)} %get-tuple-element.8), channel_id=1, source_target_pairs={{1,8},{3,10},{5,9},{7,11},{9,12},{11,14},{13,13},{15,15},{17,24},{... | collective-permute-start | bytes 786440 | tf_op jit(solution)/shard_map/ppermute | solution.py:153
  17.9 0.0 collective-permute-done.refs_1_.far
  17.9 0.0 collective-permute-done.1.paired
  17.9 0.0 copy-done
  17.9 0.0 copy-done.1
  17.9 0.6 %gather.1.pages_in = bf16[4,4,2,256,128]{4,3,2,1,0:T(8,128)(2,1)S(1)} custom-call(s32[4]{0:T(128)S(1)} %copy-done.1, bf16[2,512,512]{2,1,0:T(8,128)(2,1)S(1)} %copy-done, bf16[2,512,512]{2,1,0:T(8,128)(2,1)S(1)} %collective-permute-done.refs_1_.far, bf16[2,512,512]{2,1,0:T(8,128)(2,1)S(1)} %collective-permute-done.1.paired, f32[8,128]{1,0:T(8,128)S(1)} %first_here.1.after), custom_call_target="tpu_custom_call" | custom-call | tf_op jit(solution)/shard_map/gather/pallas_call | solution.py:189
  18.5 0.6 %attend_10.1.refs_0_ = bf16[16,8192]{1,0:T(8,128)(2,1)S(1)} custom-call(s32[4]{0:T(128)S(1)} %copy-done.1, bf16[4,4,2,256,128]{4,3,2,1,0:T(8,128)(2,1)S(1)} %gather.1.pages_in, bf16[16,8192]{1,0:T(8,128)(2,1)S(1)} %collective-permute-done.2.refs_0_.queries), custom_call_target="tpu_custom_call" | custom-call | flops 6000000000 | bytes 4194304 | tf_op jit(solution)/shard_map/attend_10/pallas_call | solution.py:201
  19.0 0.7 %collective-permute-start.8 = (bf16[16,8192]{1,0:T(8,128)(2,1)S(1)}, bf16[16,8192]{1,0:T(8,128)(2,1)S(1)}, u32[]{:S(2)}, u32[]{:S(2)}) collective-permute-start(bf16[16,8192]{1,0:T(8,128)(2,1)S(1)} %attend_10.1.refs_0_), channel_id=1, source_target_pairs={{10,0},{8,2},{11,4},{9,6},{14,8},{12,10},{15,12},{13,14},{26,16},{... | collective-permute-start | bytes 786440 | tf_op jit(solution)/shard_map/ppermute | solution.py:153
  19.7 7.8 %collective-permute-done.5.queries = bf16[16,8192]{1,0:T(8,128)(2,1)S(1)} collective-permute-done((bf16[16,8192]{1,0:T(8,128)(2,1)S(1)}, bf16[16,8192]{1,0:T(8,128)(2,1)S(1)}, u32[]{:S(2)}, u32[]{:S(2)}) %collective-permute-start.5) | collective-permute-done | bytes 262176 | tf_op jit(solution)/shard_map/ppermute | solution.py:153
  27.5 0.6 %attend_11.1.refs_0_ = bf16[16,8192]{1,0:T(8,128)(2,1)S(1)} custom-call(s32[4]{0:T(128)S(1)} %copy-done.1, bf16[4,4,2,256,128]{4,3,2,1,0:T(8,128)(2,1)S(1)} %gather.1.pages_in, bf16[16,8192]{1,0:T(8,128)(2,1)S(1)} %collective-permute-done.5.queries, bf16[16,8192]{1,0:T(8,128)(2,1)S(1)} %attend_10.1.refs_0_), custom_call_target="tpu_custom_call" | custom-call | flops 6000000000 | bytes 4194304 | tf_op jit(solution)/shard_map/attend_11/pallas_call | solution.py:201
  28.1 1.3 %collective-permute-start.9 = (bf16[16,8192]{1,0:T(8,128)(2,1)S(1)}, bf16[16,8192]{1,0:T(8,128)(2,1)S(1)}, u32[]{:S(2)}, u32[]{:S(2)}) collective-permute-start(bf16[16,8192]{1,0:T(8,128)(2,1)S(1)} %attend_11.1.refs_0_), channel_id=1, source_target_pairs={{10,1},{8,3},{11,5},{9,7},{14,9},{12,11},{15,13},{13,15},{26,17},{... | collective-permute-start | bytes 786440 | tf_op jit(solution)/shard_map/ppermute | solution.py:153
  29.4 0.0 collective-permute-done.4.queries
  29.4 0.6 %attend_00.1.refs_0_ = bf16[16,8192]{1,0:T(8,128)(2,1)S(1)} custom-call(s32[4]{0:T(128)S(1)} %copy-done.1, bf16[4,4,2,256,128]{4,3,2,1,0:T(8,128)(2,1)S(1)} %gather.1.pages_in, bf16[16,8192]{1,0:T(8,128)(2,1)S(1)} %collective-permute-done.4.queries, bf16[16,8192]{1,0:T(8,128)(2,1)S(1)} %attend_11.1.refs_0_), custom_call_target="tpu_custom_call" | custom-call | flops 6000000000 | bytes 4194304 | tf_op jit(solution)/shard_map/attend_00/pallas_call | solution.py:201
  30.0 0.7 %collective-permute-start.7 = (bf16[16,8192]{1,0:T(8,128)(2,1)S(1)}, bf16[16,8192]{1,0:T(8,128)(2,1)S(1)}, u32[]{:S(2)}, u32[]{:S(2)}) collective-permute-start(bf16[16,8192]{1,0:T(8,128)(2,1)S(1)} %attend_00.1.refs_0_), channel_id=1, source_target_pairs={{8,0},{10,2},{9,4},{11,6},{12,8},{14,10},{13,12},{15,14},{24,16},{... | collective-permute-start | bytes 786440 | tf_op jit(solution)/shard_map/ppermute | solution.py:153
  30.7 0.2 collective-permute-done.3.queries
  30.9 0.8 %attend_01.1 = bf16[16,8192]{1,0:T(8,128)(2,1)S(1)} custom-call(s32[4]{0:T(128)S(1)} %copy-done.1, bf16[4,4,2,256,128]{4,3,2,1,0:T(8,128)(2,1)S(1)} %gather.1.pages_in, bf16[16,8192]{1,0:T(8,128)(2,1)S(1)} %collective-permute-done.3.queries, bf16[16,8192]{1,0:T(8,128)(2,1)S(1)} %attend_00.1.refs_0_), custom_call_target="tpu_custom_call" | custom-call | flops 6000000000 | bytes 4194304 | tf_op jit(solution)/shard_map/attend_01/pallas_call | solution.py:201
  31.7 1.3 %collective-permute-start.6 = (bf16[16,8192]{1,0:T(8,128)(2,1)S(1)}, bf16[16,8192]{1,0:T(8,128)(2,1)S(1)}, u32[]{:S(2)}, u32[]{:S(2)}) collective-permute-start(bf16[16,8192]{1,0:T(8,128)(2,1)S(1)} %attend_01.1), channel_id=1, source_target_pairs={{8,1},{10,3},{9,5},{11,7},{12,9},{14,11},{13,13},{15,15},{24,17},{... | collective-permute-start | bytes 786440 | tf_op jit(solution)/shard_map/ppermute | solution.py:153
  33.0 7.1 %collective-permute-done.9.refs_1_ = bf16[16,8192]{1,0:T(8,128)(2,1)S(1)} collective-permute-done((bf16[16,8192]{1,0:T(8,128)(2,1)S(1)}, bf16[16,8192]{1,0:T(8,128)(2,1)S(1)}, u32[]{:S(2)}, u32[]{:S(2)}) %collective-permute-start.9) | collective-permute-done | bytes 262176 | tf_op jit(solution)/shard_map/ppermute | solution.py:153
  40.1 0.0 collective-permute-done.8.refs_0_
  40.1 0.7 %join.3.refs_1_ = bf16[16,16384]{1,0:T(8,128)(2,1)} custom-call(bf16[16,8192]{1,0:T(8,128)(2,1)S(1)} %collective-permute-done.8.refs_0_, bf16[16,8192]{1,0:T(8,128)(2,1)S(1)} %collective-permute-done.9.refs_1_), custom_call_target="tpu_custom_call" | custom-call | tf_op jit(solution)/shard_map/join/pallas_call | solution.py:216
  40.8 0.0 collective-permute-done.7.refs_0_
  40.8 5.7 %collective-permute-done.6.refs_0_ = bf16[16,8192]{1,0:T(8,128)(2,1)S(1)} collective-permute-done((bf16[16,8192]{1,0:T(8,128)(2,1)S(1)}, bf16[16,8192]{1,0:T(8,128)(2,1)S(1)}, u32[]{:S(2)}, u32[]{:S(2)}) %collective-permute-start.6) | collective-permute-done | bytes 262176 | tf_op jit(solution)/shard_map/ppermute | solution.py:153
  46.6 0.7 %join.5 = bf16[16,16384]{1,0:T(8,128)(2,1)} custom-call(bf16[16,8192]{1,0:T(8,128)(2,1)S(1)} %collective-permute-done.6.refs_0_, bf16[16,16384]{1,0:T(8,128)(2,1)} %join.4.refs_1_), custom_call_target="tpu_custom_call", output_to_operand_aliasing={{}: (1, {})} | custom-call | tf_op jit(solution)/shard_map/join/pallas_call | solution.py:216
  (2 shorter events, 0.0 us)
Async XLA Ops:
  0.0 17.9 %collective-permute-start = (bf16[2,512,512]{2,1,0:T(8,128)(2,1)}, bf16[2,512,512]{2,1,0:T(8,128)(2,1)S(1)}, u32[]{:S(2)}, u32[]{:S(2)}) collective-permute-start(bf16[2,512,512]{2,1,0:T(8,128)(2,1)} %own.1), channel_id=1, source_target_pairs={{9,12},{11,14},{12,9},{14,11},{25,28},{27,30},{28,25},{30,27}} | collective-permute-start | bytes 3145736 | tf_op jit(solution)/shard_map/ppermute | solution.py:153
  1.8 12.2 %collective-permute-start.2 = (bf16[16,8192]{1,0:T(8,128)(2,1)S(1)}, bf16[16,8192]{1,0:T(8,128)(2,1)S(1)}, u32[]{:S(2)}, u32[]{:S(2)}) collective-permute-start(bf16[16,8192]{1,0:T(8,128)(2,1)S(1)} %get-tuple-element.7), channel_id=1, source_target_pairs={{0,10},{2,8},{4,11},{6,9},{8,14},{10,12},{12,15},{14,13},{16,26},{... | collective-permute-start | bytes 786440 | tf_op jit(solution)/shard_map/ppermute | solution.py:153
  2.5 15.4 %collective-permute-start.1 = (bf16[2,512,512]{2,1,0:T(8,128)(2,1)}, bf16[2,512,512]{2,1,0:T(8,128)(2,1)S(1)}, u32[]{:S(2)}, u32[]{:S(2)}) collective-permute-start(bf16[2,512,512]{2,1,0:T(8,128)(2,1)} %own.1), channel_id=1, source_target_pairs={{8,9},{9,8},{10,11},{11,10},{12,13},{13,12},{14,15},{15,14},{24,25... | collective-permute-start | bytes 3145736 | tf_op jit(solution)/shard_map/ppermute | solution.py:153
  3.2 24.3 %collective-permute-start.5 = (bf16[16,8192]{1,0:T(8,128)(2,1)S(1)}, bf16[16,8192]{1,0:T(8,128)(2,1)S(1)}, u32[]{:S(2)}, u32[]{:S(2)}) collective-permute-start(bf16[16,8192]{1,0:T(8,128)(2,1)S(1)} %get-tuple-element.7), channel_id=1, source_target_pairs={{1,10},{3,8},{5,11},{7,9},{9,14},{11,12},{13,15},{15,13},{17,26},{... | collective-permute-start | bytes 786440 | tf_op jit(solution)/shard_map/ppermute | solution.py:153
  13.2 4.7 %copy-start = (bf16[2,512,512]{2,1,0:T(8,128)(2,1)S(1)}, bf16[2,512,512]{2,1,0:T(8,128)(2,1)}, u32[]{:S(2)}) copy-start(bf16[2,512,512]{2,1,0:T(8,128)(2,1)} %own.1) | copy-start | bytes 3145732
  13.2 4.7 %copy-start.1 = (s32[4]{0:T(128)S(1)}, s32[4]{0:T(128)}, u32[]{:S(2)}) copy-start(s32[4]{0:T(128)} %counts.9) | copy-start | bytes 52
  13.2 16.2 %collective-permute-start.4 = (bf16[16,8192]{1,0:T(8,128)(2,1)S(1)}, bf16[16,8192]{1,0:T(8,128)(2,1)S(1)}, u32[]{:S(2)}, u32[]{:S(2)}) collective-permute-start(bf16[16,8192]{1,0:T(8,128)(2,1)S(1)} %get-tuple-element.8), channel_id=1, source_target_pairs={{0,8},{2,10},{4,9},{6,11},{8,12},{10,14},{12,13},{14,15},{16,24},{... | collective-permute-start | bytes 786440 | tf_op jit(solution)/shard_map/ppermute | solution.py:153
  14.0 16.9 %collective-permute-start.3 = (bf16[16,8192]{1,0:T(8,128)(2,1)S(1)}, bf16[16,8192]{1,0:T(8,128)(2,1)S(1)}, u32[]{:S(2)}, u32[]{:S(2)}) collective-permute-start(bf16[16,8192]{1,0:T(8,128)(2,1)S(1)} %get-tuple-element.8), channel_id=1, source_target_pairs={{1,8},{3,10},{5,9},{7,11},{9,12},{11,14},{13,13},{15,15},{17,24},{... | collective-permute-start | bytes 786440 | tf_op jit(solution)/shard_map/ppermute | solution.py:153
  19.0 21.0 %collective-permute-start.8 = (bf16[16,8192]{1,0:T(8,128)(2,1)S(1)}, bf16[16,8192]{1,0:T(8,128)(2,1)S(1)}, u32[]{:S(2)}, u32[]{:S(2)}) collective-permute-start(bf16[16,8192]{1,0:T(8,128)(2,1)S(1)} %attend_10.1.refs_0_), channel_id=1, source_target_pairs={{10,0},{8,2},{11,4},{9,6},{14,8},{12,10},{15,12},{13,14},{26,16},{... | collective-permute-start | bytes 786440 | tf_op jit(solution)/shard_map/ppermute | solution.py:153
  28.1 12.0 %collective-permute-start.9 = (bf16[16,8192]{1,0:T(8,128)(2,1)S(1)}, bf16[16,8192]{1,0:T(8,128)(2,1)S(1)}, u32[]{:S(2)}, u32[]{:S(2)}) collective-permute-start(bf16[16,8192]{1,0:T(8,128)(2,1)S(1)} %attend_11.1.refs_0_), channel_id=1, source_target_pairs={{10,1},{8,3},{11,5},{9,7},{14,9},{12,11},{15,13},{13,15},{26,17},{... | collective-permute-start | bytes 786440 | tf_op jit(solution)/shard_map/ppermute | solution.py:153
  30.0 10.8 %collective-permute-start.7 = (bf16[16,8192]{1,0:T(8,128)(2,1)S(1)}, bf16[16,8192]{1,0:T(8,128)(2,1)S(1)}, u32[]{:S(2)}, u32[]{:S(2)}) collective-permute-start(bf16[16,8192]{1,0:T(8,128)(2,1)S(1)} %attend_00.1.refs_0_), channel_id=1, source_target_pairs={{8,0},{10,2},{9,4},{11,6},{12,8},{14,10},{13,12},{15,14},{24,16},{... | collective-permute-start | bytes 786440 | tf_op jit(solution)/shard_map/ppermute | solution.py:153
  31.7 14.8 %collective-permute-start.6 = (bf16[16,8192]{1,0:T(8,128)(2,1)S(1)}, bf16[16,8192]{1,0:T(8,128)(2,1)S(1)}, u32[]{:S(2)}, u32[]{:S(2)}) collective-permute-start(bf16[16,8192]{1,0:T(8,128)(2,1)S(1)} %attend_01.1), channel_id=1, source_target_pairs={{8,1},{10,3},{9,5},{11,7},{12,9},{14,11},{13,13},{15,15},{24,17},{... | collective-permute-start | bytes 786440 | tf_op jit(solution)/shard_map/ppermute | solution.py:153
where the time goes:
time: 47.7 us; the launch traced here: 47.4 us
  waiting for transfers between devices  20.9 us (44%)
  starting transfers between devices  20.7 us (43%)
  Pallas kernels  5.51 us (12%)
    ppermute x10, waiting for transfers between devices, moved(): lax.ppermute(array, ('ctx', 'head', 'sub'), [(flat(a), flat(b)) for a, b...  20.9 us
    ppermute x10, starting transfers between devices, moved(): lax.ppermute(array, ('ctx', 'head', 'sub'), [(flat(a), flat(b)) for a, b...  20.7 us
    pallas_call x4, Pallas kernels, one_request_each(): pl.pallas_call(functools.partial(attend_kernel, low_ctx, sub_size, step,...  2.45 us
    pallas_call x3, Pallas kernels, one_request_each(): pl.pallas_call(functools.partial(join_kernel, keys), out_shape=pltpu.HBM(...  1.45 us
    pallas_call x1, Pallas kernels, one_request_each(): pl.pallas_call(split_kernel, out_shape=[q_piece] * head_count, in_specs=[...  1.06 us
  transfers between devices with their start and end apart: 10, of which 4 were waited for; matrix products, arithmetic and copies ran while one was open for 0% of the time, Pallas kernels for 10%

commit v1 on v0

--- a/solution.py
+++ b/solution.py
@@ -180,12 +180,12 @@
     first_here = pl.pallas_call(
         lambda *refs: None,
         out_shape=pltpu.VMEM((8, HD), jnp.float32),
-        in_specs=[anywhere] * 2,
+        in_specs=[anywhere],
         out_specs=anywhere,
         cost_estimate=pl.CostEstimate(flops=2 * 10**10, bytes_accessed=2**20, transcendentals=0),
         compiler_params=pltpu.CompilerParams(vmem_limit_bytes=2**20),
         name="first_here",
-    )(vmem(q_in[first]), vmem(far))
+    )(vmem(q_in[first]))
     gathered = pl.pallas_call(
         functools.partial(gather_kernel, low_ctx, sub_size),
         out_shape=pltpu.VMEM((local_kv, most_pages, 2, PAGE, HD), kv_cache.dtype),

time: 47.7 us -> 48.3 us (1.013)
  waiting for transfers between devices: 20.9 us -> 23.1 us
  starting transfers between devices: 20.7 us -> 19 us
    ppermute x10, waiting for transfers between devices: 20.9 us -> 23.1 us  [moved(): lax.ppermute(array, ('ctx', 'head', 'sub'), [(flat(a), flat(b)) for a, b...]
    ppermute x10, starting transfers between devices: 20.7 us -> 19 us  [moved(): lax.ppermute(array, ('ctx', 'head', 'sub'), [(flat(a), flat(b)) for a, b...]
  transfers between devices with their start and end apart: 10 -> 10, of which waited for: 4 -> 4; matrix products, arithmetic and copies ran while one was open for 0% -> 0% of each run, Pallas kernels for 10% -> 8%
where the time goes in v1:
time: 48.3 us; the launch traced here: 48.1 us
  waiting for transfers between devices  23.1 us (48%)
  starting transfers between devices  19 us (39%)
  Pallas kernels  5.5 us (11%)
    ppermute x10, waiting for transfers between devices, moved(): lax.ppermute(array, ('ctx', 'head', 'sub'), [(flat(a), flat(b)) for a, b...  23.1 us
    ppermute x10, starting transfers between devices, moved(): lax.ppermute(array, ('ctx', 'head', 'sub'), [(flat(a), flat(b)) for a, b...  19 us
    pallas_call x4, Pallas kernels, one_request_each(): pl.pallas_call(functools.partial(attend_kernel, low_ctx, sub_size, step,...  2.45 us
    pallas_call x3, Pallas kernels, one_request_each(): pl.pallas_call(functools.partial(join_kernel, keys), out_shape=pltpu.HBM(...  1.45 us
    pallas_call x1, Pallas kernels, one_request_each(): pl.pallas_call(split_kernel, out_shape=[q_piece] * head_count, in_specs=[...  1.04 us
  transfers between devices with their start and end apart: 10, of which 4 were waited for; matrix products, arithmetic and copies ran while one was open for 0% of the time, Pallas kernels for 8%

profile of v1, /device:TPU:13, one launch (start us, length us, event | category | flops | bytes accessed | tf_op | source)
XLA Modules:
  0.0 48.1 jit_solution(10907787756375276651)
XLA Ops:
  0.0 1.0 %split.1 = (bf16[16,8192]{1,0:T(8,128)(2,1)S(1)}, bf16[16,8192]{1,0:T(8,128)(2,1)S(1)}) custom-call(bf16[16,16384]{1,0:T(8,128)(2,1)} %queries.1), custom_call_target="tpu_custom_call" | custom-call | tf_op jit(solution)/shard_map/split/pallas_call | solution.py:159
  1.1 0.7 %collective-permute-start.2 = (bf16[16,8192]{1,0:T(8,128)(2,1)S(1)}, bf16[16,8192]{1,0:T(8,128)(2,1)S(1)}, u32[]{:S(2)}, u32[]{:S(2)}) collective-permute-start(bf16[16,8192]{1,0:T(8,128)(2,1)S(1)} %get-tuple-element.7), channel_id=1, source_target_pairs={{0,10},{2,8},{4,11},{6,9},{8,14},{10,12},{12,15},{14,13},{16,26},{... | collective-permute-start | bytes 786440 | tf_op jit(solution)/shard_map/ppermute | solution.py:153
  1.7 0.7 %collective-permute-start = (bf16[2,512,512]{2,1,0:T(8,128)(2,1)}, bf16[2,512,512]{2,1,0:T(8,128)(2,1)S(1)}, u32[]{:S(2)}, u32[]{:S(2)}) collective-permute-start(bf16[2,512,512]{2,1,0:T(8,128)(2,1)} %own.1), channel_id=1, source_target_pairs={{9,12},{11,14},{12,9},{14,11},{25,28},{27,30},{28,25},{30,27}} | collective-permute-start | bytes 3145736 | tf_op jit(solution)/shard_map/ppermute | solution.py:153
  2.5 0.7 %collective-permute-start.1 = (bf16[2,512,512]{2,1,0:T(8,128)(2,1)}, bf16[2,512,512]{2,1,0:T(8,128)(2,1)S(1)}, u32[]{:S(2)}, u32[]{:S(2)}) collective-permute-start(bf16[2,512,512]{2,1,0:T(8,128)(2,1)} %own.1), channel_id=1, source_target_pairs={{8,9},{9,8},{10,11},{11,10},{12,13},{13,12},{14,15},{15,14},{24,25... | collective-permute-start | bytes 3145736 | tf_op jit(solution)/shard_map/ppermute | solution.py:153
  3.2 9.6 %collective-permute-start.5 = (bf16[16,8192]{1,0:T(8,128)(2,1)S(1)}, bf16[16,8192]{1,0:T(8,128)(2,1)S(1)}, u32[]{:S(2)}, u32[]{:S(2)}) collective-permute-start(bf16[16,8192]{1,0:T(8,128)(2,1)S(1)} %get-tuple-element.7), channel_id=1, source_target_pairs={{1,10},{3,8},{5,11},{7,9},{9,14},{11,12},{13,15},{15,13},{17,26},{... | collective-permute-start | bytes 786440 | tf_op jit(solution)/shard_map/ppermute | solution.py:153
  12.8 0.0 copy-start
  12.9 0.0 copy-start.1
  12.9 0.8 %collective-permute-start.4 = (bf16[16,8192]{1,0:T(8,128)(2,1)S(1)}, bf16[16,8192]{1,0:T(8,128)(2,1)S(1)}, u32[]{:S(2)}, u32[]{:S(2)}) collective-permute-start(bf16[16,8192]{1,0:T(8,128)(2,1)S(1)} %get-tuple-element.8), channel_id=1, source_target_pairs={{0,8},{2,10},{4,9},{6,11},{8,12},{10,14},{12,13},{14,15},{16,24},{... | collective-permute-start | bytes 786440 | tf_op jit(solution)/shard_map/ppermute | solution.py:153
  13.7 0.0 collective-permute-done.2.refs_0_.queries
  13.7 2.5 %collective-permute-start.3 = (bf16[16,8192]{1,0:T(8,128)(2,1)S(1)}, bf16[16,8192]{1,0:T(8,128)(2,1)S(1)}, u32[]{:S(2)}, u32[]{:S(2)}) collective-permute-start(bf16[16,8192]{1,0:T(8,128)(2,1)S(1)} %get-tuple-element.8), channel_id=1, source_target_pairs={{1,8},{3,10},{5,9},{7,11},{9,12},{11,14},{13,13},{15,15},{17,24},{... | collective-permute-start | bytes 786440 | tf_op jit(solution)/shard_map/ppermute | solution.py:153
  16.2 0.0 collective-permute-done.far
  16.3 0.0 collective-permute-done.1.paired
  16.3 0.0 copy-done
  16.3 0.0 copy-done.1
  16.3 0.6 %gather.1.pages_in = bf16[4,4,2,256,128]{4,3,2,1,0:T(8,128)(2,1)S(1)} custom-call(s32[4]{0:T(128)S(1)} %copy-done.1, bf16[2,512,512]{2,1,0:T(8,128)(2,1)S(1)} %copy-done, bf16[2,512,512]{2,1,0:T(8,128)(2,1)S(1)} %collective-permute-done.far, bf16[2,512,512]{2,1,0:T(8,128)(2,1)S(1)} %collective-permute-done.1.paired, f32[8,128]{1,0:T(8,128)S(1)} %first_here.1.after), custom_call_target="tpu_custom_call" | custom-call | tf_op jit(solution)/shard_map/gather/pallas_call | solution.py:189
  16.8 0.6 %attend_10.1.refs_0_ = bf16[16,8192]{1,0:T(8,128)(2,1)S(1)} custom-call(s32[4]{0:T(128)S(1)} %copy-done.1, bf16[4,4,2,256,128]{4,3,2,1,0:T(8,128)(2,1)S(1)} %gather.1.pages_in, bf16[16,8192]{1,0:T(8,128)(2,1)S(1)} %collective-permute-done.2.refs_0_.queries), custom_call_target="tpu_custom_call" | custom-call | flops 6000000000 | bytes 4194304 | tf_op jit(solution)/shard_map/attend_10/pallas_call | solution.py:201
  17.4 0.7 %collective-permute-start.8 = (bf16[16,8192]{1,0:T(8,128)(2,1)S(1)}, bf16[16,8192]{1,0:T(8,128)(2,1)S(1)}, u32[]{:S(2)}, u32[]{:S(2)}) collective-permute-start(bf16[16,8192]{1,0:T(8,128)(2,1)S(1)} %attend_10.1.refs_0_), channel_id=1, source_target_pairs={{10,0},{8,2},{11,4},{9,6},{14,8},{12,10},{15,12},{13,14},{26,16},{... | collective-permute-start | bytes 786440 | tf_op jit(solution)/shard_map/ppermute | solution.py:153
  18.1 7.8 %collective-permute-done.5.queries = bf16[16,8192]{1,0:T(8,128)(2,1)S(1)} collective-permute-done((bf16[16,8192]{1,0:T(8,128)(2,1)S(1)}, bf16[16,8192]{1,0:T(8,128)(2,1)S(1)}, u32[]{:S(2)}, u32[]{:S(2)}) %collective-permute-start.5) | collective-permute-done | bytes 262176 | tf_op jit(solution)/shard_map/ppermute | solution.py:153
  25.9 0.6 %attend_11.1.refs_0_ = bf16[16,8192]{1,0:T(8,128)(2,1)S(1)} custom-call(s32[4]{0:T(128)S(1)} %copy-done.1, bf16[4,4,2,256,128]{4,3,2,1,0:T(8,128)(2,1)S(1)} %gather.1.pages_in, bf16[16,8192]{1,0:T(8,128)(2,1)S(1)} %collective-permute-done.5.queries, bf16[16,8192]{1,0:T(8,128)(2,1)S(1)} %attend_10.1.refs_0_), custom_call_target="tpu_custom_call" | custom-call | flops 6000000000 | bytes 4194304 | tf_op jit(solution)/shard_map/attend_11/pallas_call | solution.py:201
  26.5 1.3 %collective-permute-start.9 = (bf16[16,8192]{1,0:T(8,128)(2,1)S(1)}, bf16[16,8192]{1,0:T(8,128)(2,1)S(1)}, u32[]{:S(2)}, u32[]{:S(2)}) collective-permute-start(bf16[16,8192]{1,0:T(8,128)(2,1)S(1)} %attend_11.1.refs_0_), channel_id=1, source_target_pairs={{10,1},{8,3},{11,5},{9,7},{14,9},{12,11},{15,13},{13,15},{26,17},{... | collective-permute-start | bytes 786440 | tf_op jit(solution)/shard_map/ppermute | solution.py:153
  27.8 0.0 collective-permute-done.4.queries
  27.8 0.6 %attend_00.1.refs_0_ = bf16[16,8192]{1,0:T(8,128)(2,1)S(1)} custom-call(s32[4]{0:T(128)S(1)} %copy-done.1, bf16[4,4,2,256,128]{4,3,2,1,0:T(8,128)(2,1)S(1)} %gather.1.pages_in, bf16[16,8192]{1,0:T(8,128)(2,1)S(1)} %collective-permute-done.4.queries, bf16[16,8192]{1,0:T(8,128)(2,1)S(1)} %attend_11.1.refs_0_), custom_call_target="tpu_custom_call" | custom-call | flops 6000000000 | bytes 4194304 | tf_op jit(solution)/shard_map/attend_00/pallas_call | solution.py:201
  28.3 0.7 %collective-permute-start.7 = (bf16[16,8192]{1,0:T(8,128)(2,1)S(1)}, bf16[16,8192]{1,0:T(8,128)(2,1)S(1)}, u32[]{:S(2)}, u32[]{:S(2)}) collective-permute-start(bf16[16,8192]{1,0:T(8,128)(2,1)S(1)} %attend_00.1.refs_0_), channel_id=1, source_target_pairs={{8,0},{10,2},{9,4},{11,6},{12,8},{14,10},{13,12},{15,14},{24,16},{... | collective-permute-start | bytes 786440 | tf_op jit(solution)/shard_map/ppermute | solution.py:153
  29.0 1.1 %collective-permute-done.3.queries = bf16[16,8192]{1,0:T(8,128)(2,1)S(1)} collective-permute-done((bf16[16,8192]{1,0:T(8,128)(2,1)S(1)}, bf16[16,8192]{1,0:T(8,128)(2,1)S(1)}, u32[]{:S(2)}, u32[]{:S(2)}) %collective-permute-start.3) | collective-permute-done | bytes 262176 | tf_op jit(solution)/shard_map/ppermute | solution.py:153
  30.2 0.8 %attend_01.1 = bf16[16,8192]{1,0:T(8,128)(2,1)S(1)} custom-call(s32[4]{0:T(128)S(1)} %copy-done.1, bf16[4,4,2,256,128]{4,3,2,1,0:T(8,128)(2,1)S(1)} %gather.1.pages_in, bf16[16,8192]{1,0:T(8,128)(2,1)S(1)} %collective-permute-done.3.queries, bf16[16,8192]{1,0:T(8,128)(2,1)S(1)} %attend_00.1.refs_0_), custom_call_target="tpu_custom_call" | custom-call | flops 6000000000 | bytes 4194304 | tf_op jit(solution)/shard_map/attend_01/pallas_call | solution.py:201
  31.0 1.3 %collective-permute-start.6 = (bf16[16,8192]{1,0:T(8,128)(2,1)S(1)}, bf16[16,8192]{1,0:T(8,128)(2,1)S(1)}, u32[]{:S(2)}, u32[]{:S(2)}) collective-permute-start(bf16[16,8192]{1,0:T(8,128)(2,1)S(1)} %attend_01.1), channel_id=1, source_target_pairs={{8,1},{10,3},{9,5},{11,7},{12,9},{14,11},{13,13},{15,15},{24,17},{... | collective-permute-start | bytes 786440 | tf_op jit(solution)/shard_map/ppermute | solution.py:153
  32.3 7.4 %collective-permute-done.9.refs_1_ = bf16[16,8192]{1,0:T(8,128)(2,1)S(1)} collective-permute-done((bf16[16,8192]{1,0:T(8,128)(2,1)S(1)}, bf16[16,8192]{1,0:T(8,128)(2,1)S(1)}, u32[]{:S(2)}, u32[]{:S(2)}) %collective-permute-start.9) | collective-permute-done | bytes 262176 | tf_op jit(solution)/shard_map/ppermute | solution.py:153
  39.6 0.0 collective-permute-done.8.refs_0_
  39.6 0.7 %join.3.refs_1_ = bf16[16,16384]{1,0:T(8,128)(2,1)} custom-call(bf16[16,8192]{1,0:T(8,128)(2,1)S(1)} %collective-permute-done.8.refs_0_, bf16[16,8192]{1,0:T(8,128)(2,1)S(1)} %collective-permute-done.9.refs_1_), custom_call_target="tpu_custom_call" | custom-call | tf_op jit(solution)/shard_map/join/pallas_call | solution.py:216
  40.4 0.0 collective-permute-done.7.refs_0_
  40.4 6.8 %collective-permute-done.6.refs_0_ = bf16[16,8192]{1,0:T(8,128)(2,1)S(1)} collective-permute-done((bf16[16,8192]{1,0:T(8,128)(2,1)S(1)}, bf16[16,8192]{1,0:T(8,128)(2,1)S(1)}, u32[]{:S(2)}, u32[]{:S(2)}) %collective-permute-start.6) | collective-permute-done | bytes 262176 | tf_op jit(solution)/shard_map/ppermute | solution.py:153
  47.2 0.7 %join.5 = bf16[16,16384]{1,0:T(8,128)(2,1)} custom-call(bf16[16,8192]{1,0:T(8,128)(2,1)S(1)} %collective-permute-done.6.refs_0_, bf16[16,16384]{1,0:T(8,128)(2,1)} %join.4.refs_1_), custom_call_target="tpu_custom_call", output_to_operand_aliasing={{}: (1, {})} | custom-call | tf_op jit(solution)/shard_map/join/pallas_call | solution.py:216
  (2 shorter events, 0.0 us)
Async XLA Ops:
  1.1 12.6 %collective-permute-start.2 = (bf16[16,8192]{1,0:T(8,128)(2,1)S(1)}, bf16[16,8192]{1,0:T(8,128)(2,1)S(1)}, u32[]{:S(2)}, u32[]{:S(2)}) collective-permute-start(bf16[16,8192]{1,0:T(8,128)(2,1)S(1)} %get-tuple-element.7), channel_id=1, source_target_pairs={{0,10},{2,8},{4,11},{6,9},{8,14},{10,12},{12,15},{14,13},{16,26},{... | collective-permute-start | bytes 786440 | tf_op jit(solution)/shard_map/ppermute | solution.py:153
  1.7 14.5 %collective-permute-start = (bf16[2,512,512]{2,1,0:T(8,128)(2,1)}, bf16[2,512,512]{2,1,0:T(8,128)(2,1)S(1)}, u32[]{:S(2)}, u32[]{:S(2)}) collective-permute-start(bf16[2,512,512]{2,1,0:T(8,128)(2,1)} %own.1), channel_id=1, source_target_pairs={{9,12},{11,14},{12,9},{14,11},{25,28},{27,30},{28,25},{30,27}} | collective-permute-start | bytes 3145736 | tf_op jit(solution)/shard_map/ppermute | solution.py:153
  2.5 13.8 %collective-permute-start.1 = (bf16[2,512,512]{2,1,0:T(8,128)(2,1)}, bf16[2,512,512]{2,1,0:T(8,128)(2,1)S(1)}, u32[]{:S(2)}, u32[]{:S(2)}) collective-permute-start(bf16[2,512,512]{2,1,0:T(8,128)(2,1)} %own.1), channel_id=1, source_target_pairs={{8,9},{9,8},{10,11},{11,10},{12,13},{13,12},{14,15},{15,14},{24,25... | collective-permute-start | bytes 3145736 | tf_op jit(solution)/shard_map/ppermute | solution.py:153
  3.2 22.7 %collective-permute-start.5 = (bf16[16,8192]{1,0:T(8,128)(2,1)S(1)}, bf16[16,8192]{1,0:T(8,128)(2,1)S(1)}, u32[]{:S(2)}, u32[]{:S(2)}) collective-permute-start(bf16[16,8192]{1,0:T(8,128)(2,1)S(1)} %get-tuple-element.7), channel_id=1, source_target_pairs={{1,10},{3,8},{5,11},{7,9},{9,14},{11,12},{13,15},{15,13},{17,26},{... | collective-permute-start | bytes 786440 | tf_op jit(solution)/shard_map/ppermute | solution.py:153
  12.8 3.4 %copy-start = (bf16[2,512,512]{2,1,0:T(8,128)(2,1)S(1)}, bf16[2,512,512]{2,1,0:T(8,128)(2,1)}, u32[]{:S(2)}) copy-start(bf16[2,512,512]{2,1,0:T(8,128)(2,1)} %own.1) | copy-start | bytes 3145732
  12.9 3.4 %copy-start.1 = (s32[4]{0:T(128)S(1)}, s32[4]{0:T(128)}, u32[]{:S(2)}) copy-start(s32[4]{0:T(128)} %counts.9) | copy-start | bytes 52
  12.9 14.9 %collective-permute-start.4 = (bf16[16,8192]{1,0:T(8,128)(2,1)S(1)}, bf16[16,8192]{1,0:T(8,128)(2,1)S(1)}, u32[]{:S(2)}, u32[]{:S(2)}) collective-permute-start(bf16[16,8192]{1,0:T(8,128)(2,1)S(1)} %get-tuple-element.8), channel_id=1, source_target_pairs={{0,8},{2,10},{4,9},{6,11},{8,12},{10,14},{12,13},{14,15},{16,24},{... | collective-permute-start | bytes 786440 | tf_op jit(solution)/shard_map/ppermute | solution.py:153
  13.7 16.5 %collective-permute-start.3 = (bf16[16,8192]{1,0:T(8,128)(2,1)S(1)}, bf16[16,8192]{1,0:T(8,128)(2,1)S(1)}, u32[]{:S(2)}, u32[]{:S(2)}) collective-permute-start(bf16[16,8192]{1,0:T(8,128)(2,1)S(1)} %get-tuple-element.8), channel_id=1, source_target_pairs={{1,8},{3,10},{5,9},{7,11},{9,12},{11,14},{13,13},{15,15},{17,24},{... | collective-permute-start | bytes 786440 | tf_op jit(solution)/shard_map/ppermute | solution.py:153
  17.4 22.2 %collective-permute-start.8 = (bf16[16,8192]{1,0:T(8,128)(2,1)S(1)}, bf16[16,8192]{1,0:T(8,128)(2,1)S(1)}, u32[]{:S(2)}, u32[]{:S(2)}) collective-permute-start(bf16[16,8192]{1,0:T(8,128)(2,1)S(1)} %attend_10.1.refs_0_), channel_id=1, source_target_pairs={{10,0},{8,2},{11,4},{9,6},{14,8},{12,10},{15,12},{13,14},{26,16},{... | collective-permute-start | bytes 786440 | tf_op jit(solution)/shard_map/ppermute | solution.py:153
  26.5 13.2 %collective-permute-start.9 = (bf16[16,8192]{1,0:T(8,128)(2,1)S(1)}, bf16[16,8192]{1,0:T(8,128)(2,1)S(1)}, u32[]{:S(2)}, u32[]{:S(2)}) collective-permute-start(bf16[16,8192]{1,0:T(8,128)(2,1)S(1)} %attend_11.1.refs_0_), channel_id=1, source_target_pairs={{10,1},{8,3},{11,5},{9,7},{14,9},{12,11},{15,13},{13,15},{26,17},{... | collective-permute-start | bytes 786440 | tf_op jit(solution)/shard_map/ppermute | solution.py:153
  28.3 12.0 %collective-permute-start.7 = (bf16[16,8192]{1,0:T(8,128)(2,1)S(1)}, bf16[16,8192]{1,0:T(8,128)(2,1)S(1)}, u32[]{:S(2)}, u32[]{:S(2)}) collective-permute-start(bf16[16,8192]{1,0:T(8,128)(2,1)S(1)} %attend_00.1.refs_0_), channel_id=1, source_target_pairs={{8,0},{10,2},{9,4},{11,6},{12,8},{14,10},{13,12},{15,14},{24,16},{... | collective-permute-start | bytes 786440 | tf_op jit(solution)/shard_map/ppermute | solution.py:153
  31.0 16.2 %collective-permute-start.6 = (bf16[16,8192]{1,0:T(8,128)(2,1)S(1)}, bf16[16,8192]{1,0:T(8,128)(2,1)S(1)}, u32[]{:S(2)}, u32[]{:S(2)}) collective-permute-start(bf16[16,8192]{1,0:T(8,128)(2,1)S(1)} %attend_01.1), channel_id=1, source_target_pairs={{8,1},{10,3},{9,5},{11,7},{12,9},{14,11},{13,13},{15,15},{24,17},{... | collective-permute-start | bytes 786440 | tf_op jit(solution)/shard_map/ppermute | solution.py:153

commit v2 on v0

--- a/solution.py
+++ b/solution.py
@@ -39,12 +39,15 @@
     ])
 
 
-def join_kernel(keys, *refs):
+def join_kernel(low_ctx, turns, *refs):
     out, sems = refs[-2:]
-    for i, (step, source) in enumerate(keys):
-        @pl.when(lax.axis_index("sub") == source)
-        def _():
-            run([pltpu.make_async_copy(refs[i], out.at[:, head_part(step, refs[i].shape[1])], sems.at[0])])
+    is_lower = lax.axis_index("ctx") < low_ctx
+    for piece, keys in zip(refs, turns):
+        for key, here in zip(keys, (is_lower, jnp.logical_not(is_lower))):
+            if key is not None:
+                @pl.when(here & (lax.axis_index("sub") == key[1]))
+                def _():
+                    run([pltpu.make_async_copy(piece, out.at[:, head_part(key[0], piece.shape[1])], sems.at[0])])
 
 
 def own_pair_of(low_ctx, sub_count):
@@ -75,7 +78,7 @@
                             out[g, p, i] = ref[i, page_rows, g * HD:(g + 1) * HD]
 
 
-def attend_kernel(low_ctx, sub_count, step, source_sub, waits, counts, pages_in, queries, *refs):
+def attend_kernel(low_ctx, sub_count, turn, waits, counts, pages_in, queries, *refs):
     out = refs[waits]
     head = lax.axis_index("head")
     tokens, width = queries.shape
@@ -83,7 +86,21 @@
     span = width // local_kv
     per_group = span // HD
     rows = per_group * tokens
-    first_token = ((head ^ step) * sub_count + source_sub) * tokens
+    request = own_pair_of(low_ctx, sub_count)
+
+    def token_of(key):
+        return ((head ^ key[0]) * sub_count + key[1]) * tokens
+
+    lower, upper = turn
+    if lower is None or upper is None:
+        first_token = token_of(lower or upper)
+    else:
+        first_token = jnp.where(request < low_ctx, token_of(lower), token_of(upper))
+    works = (lax.axis_index("ctx") >= low_ctx)
+    if lower is None:
+        works = works & (request >= low_ctx)
+    if upper is None:
+        works = works & (request < low_ctx)
 
     def attend(pages):
         token = lax.rem(lax.broadcasted_iota(jnp.int32, (rows, PAGE), 0), tokens)
@@ -120,9 +137,9 @@
             )
             scores = later
 
-    @pl.when(lax.axis_index("ctx") >= low_ctx)
+    @pl.when(works)
     def _():
-        count = counts[own_pair_of(low_ctx, sub_count)]
+        count = counts[request]
         for pages in [*range(1, most_pages - REQS + 3), most_pages]:
             @pl.when(count == pages)
             def _():
@@ -165,12 +182,18 @@
         compiler_params=pltpu.CompilerParams(vmem_limit_bytes=2**20),
         name="split",
     )(hbm(queries))
-    routes = {
-        (step, s): [((r, h, s), worker(r, h ^ step)) for r in range(ctx_size) for h in heads]
-        for step in heads[::-1] for s in range(sub_size)
-    }
-    q_in = {key: moved(q_out[key[0]], pairs) for key, pairs in routes.items()}
-    first = list(routes)[0]
+    lower = [(step, s) for step in heads[::-1] for s in range(sub_size)]
+    upper = [lower[0]] + lower[2:] + [lower[1]]
+    turns = list(zip(lower + [None], [None] + upper))
+
+    def routes_of(turn):
+        return [
+            ((r, h, key[1]), worker(r, h ^ key[0]))
+            for key, requests in zip(turn, (range(low_ctx), range(low_ctx, ctx_size))) if key is not None
+            for r in requests for h in heads
+        ]
+
+    q_in = [moved(q_out[(turn[0] or turn[1])[0]], routes_of(turn)) for turn in turns]
 
     middle = [(low_ctx, sub_size - 1), (low_ctx + 1, 0)]
     far = moved(kv_cache, [((a[0], h, a[1]), (b[0], h, b[1])) for a, b in (middle, middle[::-1]) for h in heads])
@@ -185,7 +208,7 @@
         cost_estimate=pl.CostEstimate(flops=2 * 10**10, bytes_accessed=2**20, transcendentals=0),
         compiler_params=pltpu.CompilerParams(vmem_limit_bytes=2**20),
         name="first_here",
-    )(vmem(q_in[first]), vmem(far))
+    )(vmem(q_in[0]), vmem(far))
     gathered = pl.pallas_call(
         functools.partial(gather_kernel, low_ctx, sub_size),
         out_shape=pltpu.VMEM((local_kv, most_pages, 2, PAGE, HD), kv_cache.dtype),
@@ -195,34 +218,34 @@
         name="gather",
     )(page_counts, vmem(kv_cache), vmem(far), vmem(paired), vmem(first_here))
 
-    back = {}
+    back = []
     after = []
-    for step, s in routes:
+    for turn, arrived in zip(turns, q_in):
         out = pl.pallas_call(
-            functools.partial(attend_kernel, low_ctx, sub_size, step, s, len(after)),
+            functools.partial(attend_kernel, low_ctx, sub_size, turn, len(after)),
             out_shape=q_piece,
             in_specs=[pl.BlockSpec(memory_space=pltpu.SMEM)] + [in_vmem] * 2 + [anywhere] * len(after),
             out_specs=in_vmem,
             compiler_params=pltpu.CompilerParams(vmem_limit_bytes=12 * 2**20),
             cost_estimate=pl.CostEstimate(flops=6 * 10**9, bytes_accessed=2**22, transcendentals=10**6),
-            name=f"attend_{step}{s}",
-        )(page_counts, vmem(gathered), vmem(q_in[step, s]), *after)
-        back[step, s] = moved(out, [(b, a) for a, b in routes[step, s]])
+            name=f"attend_{len(back)}",
+        )(page_counts, vmem(gathered), vmem(arrived), *after)
+        back.append(moved(out, [(b, a) for a, b in routes_of(turn)]))
         after = [out]
 
     joined = []
-    for keys in [[key for key in routes if key[0]]] + [[key] for key in routes if not key[0]]:
+    for chosen in [range(len(turns) - 2)] + [[i] for i in range(len(turns) - 2, len(turns))]:
         joined = [
             pl.pallas_call(
-                functools.partial(join_kernel, keys),
+                functools.partial(join_kernel, low_ctx, [turns[i] for i in chosen]),
                 out_shape=pltpu.HBM(queries.shape, queries.dtype),
-                in_specs=[anywhere] * (len(keys) + len(joined)),
+                in_specs=[anywhere] * (len(chosen) + len(joined)),
                 out_specs=anywhere,
                 scratch_shapes=[pltpu.SemaphoreType.DMA((1,))],
-                input_output_aliases={len(keys): 0} if joined else {},
+                input_output_aliases={len(chosen): 0} if joined else {},
                 compiler_params=pltpu.CompilerParams(vmem_limit_bytes=2**20),
                 name="join",
-            )(*[vmem(back[key]) for key in keys], *map(hbm, joined))
+            )(*[vmem(back[i]) for i in chosen], *map(hbm, joined))
         ]
     return joined[0]
 

time: 47.7 us -> 52.6 us (1.10)
  the two profiles are of different devices: /device:TPU:13 before, /device:TPU:17 now
where the time goes in v2:
time: 52.6 us; the launch traced here: 52.3 us
  waiting for transfers between devices  21.4 us (41%)
  starting transfers between devices  20 us (38%)
  Pallas kernels  10.4 us (20%)
    ppermute x12, waiting for transfers between devices, moved(): lax.ppermute(array, ('ctx', 'head', 'sub'), [(flat(a), flat(b)) for a, b...  21.4 us
    ppermute x12, starting transfers between devices, moved(): lax.ppermute(array, ('ctx', 'head', 'sub'), [(flat(a), flat(b)) for a, b...  20 us
    pallas_call x5, Pallas kernels, one_request_each(): pl.pallas_call(functools.partial(attend_kernel, low_ctx, sub_size, turn,...  7.02 us
    pallas_call x3, Pallas kernels, one_request_each(): pl.pallas_call(functools.partial(join_kernel, low_ctx, [turns[i] for i in...  1.46 us
    pallas_call x1, Pallas kernels, one_request_each(): pl.pallas_call(split_kernel, out_shape=[q_piece] * head_count, in_specs=[...  1.06 us
  transfers between devices with their start and end apart: 12, of which 3 were waited for; matrix products, arithmetic and copies ran while one was open for 0% of the time, Pallas kernels for 18%

profile of v2, /device:TPU:17, one launch (start us, length us, event | category | flops | bytes accessed | tf_op | source)
XLA Modules:
  0.0 52.3 jit_solution(4196468903208588907)
XLA Ops:
  0.0 3.8 %collective-permute-start = (bf16[2,512,512]{2,1,0:T(8,128)(2,1)}, bf16[2,512,512]{2,1,0:T(8,128)(2,1)S(1)}, u32[]{:S(2)}, u32[]{:S(2)}) collective-permute-start(bf16[2,512,512]{2,1,0:T(8,128)(2,1)} %own.1), channel_id=1, source_target_pairs={{9,12},{11,14},{12,9},{14,11},{25,28},{27,30},{28,25},{30,27}} | collective-permute-start | bytes 3145736 | tf_op jit(solution)/shard_map/ppermute | solution.py:170
  3.8 1.1 %split.1 = (bf16[16,8192]{1,0:T(8,128)(2,1)S(1)}, bf16[16,8192]{1,0:T(8,128)(2,1)S(1)}) custom-call(bf16[16,16384]{1,0:T(8,128)(2,1)} %queries.1), custom_call_target="tpu_custom_call" | custom-call | tf_op jit(solution)/shard_map/split/pallas_call | solution.py:176
  4.8 1.3 %collective-permute-start.2 = (bf16[16,8192]{1,0:T(8,128)(2,1)S(1)}, bf16[16,8192]{1,0:T(8,128)(2,1)S(1)}, u32[]{:S(2)}, u32[]{:S(2)}) collective-permute-start(bf16[16,8192]{1,0:T(8,128)(2,1)S(1)} %get-tuple-element.7), channel_id=1, source_target_pairs={{0,10},{2,8},{4,11},{6,9},{16,26},{18,24},{20,27},{22,25}} | collective-permute-start | bytes 786440 | tf_op jit(solution)/shard_map/ppermute | solution.py:170
  6.1 1.9 %collective-permute-start.1 = (bf16[2,512,512]{2,1,0:T(8,128)(2,1)}, bf16[2,512,512]{2,1,0:T(8,128)(2,1)S(1)}, u32[]{:S(2)}, u32[]{:S(2)}) collective-permute-start(bf16[2,512,512]{2,1,0:T(8,128)(2,1)} %own.1), channel_id=1, source_target_pairs={{8,9},{9,8},{10,11},{11,10},{12,13},{13,12},{14,15},{15,14},{24,25... | collective-permute-start | bytes 3145736 | tf_op jit(solution)/shard_map/ppermute | solution.py:170
  8.1 1.3 %collective-permute-start.6 = (bf16[16,8192]{1,0:T(8,128)(2,1)S(1)}, bf16[16,8192]{1,0:T(8,128)(2,1)S(1)}, u32[]{:S(2)}, u32[]{:S(2)}) collective-permute-start(bf16[16,8192]{1,0:T(8,128)(2,1)S(1)} %get-tuple-element.7), channel_id=1, source_target_pairs={{1,10},{3,8},{5,11},{7,9},{8,14},{10,12},{12,15},{14,13},{17,26},{... | collective-permute-start | bytes 786440 | tf_op jit(solution)/shard_map/ppermute | solution.py:170
  9.4 0.0 copy-start
  9.4 0.0 copy-start.1
  9.4 1.4 %collective-permute-start.5 = (bf16[16,8192]{1,0:T(8,128)(2,1)S(1)}, bf16[16,8192]{1,0:T(8,128)(2,1)S(1)}, u32[]{:S(2)}, u32[]{:S(2)}) collective-permute-start(bf16[16,8192]{1,0:T(8,128)(2,1)S(1)} %get-tuple-element.8), channel_id=1, source_target_pairs={{0,8},{2,10},{4,9},{6,11},{8,12},{10,14},{12,13},{14,15},{16,24},{... | collective-permute-start | bytes 786440 | tf_op jit(solution)/shard_map/ppermute | solution.py:170
  10.8 13.6 %collective-permute-done.2.refs_0_.queries = bf16[16,8192]{1,0:T(8,128)(2,1)S(1)} collective-permute-done((bf16[16,8192]{1,0:T(8,128)(2,1)S(1)}, bf16[16,8192]{1,0:T(8,128)(2,1)S(1)}, u32[]{:S(2)}, u32[]{:S(2)}) %collective-permute-start.2) | collective-permute-done | bytes 262176 | tf_op jit(solution)/shard_map/ppermute | solution.py:170
  24.4 1.9 %collective-permute-start.4 = (bf16[16,8192]{1,0:T(8,128)(2,1)S(1)}, bf16[16,8192]{1,0:T(8,128)(2,1)S(1)}, u32[]{:S(2)}, u32[]{:S(2)}) collective-permute-start(bf16[16,8192]{1,0:T(8,128)(2,1)S(1)} %get-tuple-element.8), channel_id=1, source_target_pairs={{1,8},{3,10},{5,9},{7,11},{9,12},{11,14},{13,13},{15,15},{17,24},{... | collective-permute-start | bytes 786440 | tf_op jit(solution)/shard_map/ppermute | solution.py:170
  26.3 0.0 collective-permute-done.refs_1_.far
  26.3 1.3 %collective-permute-start.3 = (bf16[16,8192]{1,0:T(8,128)(2,1)S(1)}, bf16[16,8192]{1,0:T(8,128)(2,1)S(1)}, u32[]{:S(2)}, u32[]{:S(2)}) collective-permute-start(bf16[16,8192]{1,0:T(8,128)(2,1)S(1)} %get-tuple-element.7), channel_id=1, source_target_pairs={{9,14},{11,12},{13,15},{15,13},{25,30},{27,28},{29,31},{31,29}} | collective-permute-start | bytes 786440 | tf_op jit(solution)/shard_map/ppermute | solution.py:170
  27.6 0.0 collective-permute-done.1.paired
  27.6 0.0 copy-done
  27.7 0.0 copy-done.1
  27.7 0.8 %gather.1.pages_in = bf16[4,4,2,256,128]{4,3,2,1,0:T(8,128)(2,1)S(1)} custom-call(s32[4]{0:T(128)S(1)} %copy-done.1, bf16[2,512,512]{2,1,0:T(8,128)(2,1)S(1)} %copy-done, bf16[2,512,512]{2,1,0:T(8,128)(2,1)S(1)} %collective-permute-done.refs_1_.far, bf16[2,512,512]{2,1,0:T(8,128)(2,1)S(1)} %collective-permute-done.1.paired, f32[8,128]{1,0:T(8,128)S(1)} %first_here.1.after), custom_call_target="tpu_custom_call" | custom-call | tf_op jit(solution)/shard_map/gather/pallas_call | solution.py:212
  28.5 1.5 %attend_0.1.refs_0_ = bf16[16,8192]{1,0:T(8,128)(2,1)S(1)} custom-call(s32[4]{0:T(128)S(1)} %copy-done.1, bf16[4,4,2,256,128]{4,3,2,1,0:T(8,128)(2,1)S(1)} %gather.1.pages_in, bf16[16,8192]{1,0:T(8,128)(2,1)S(1)} %collective-permute-done.2.refs_0_.queries), custom_call_target="tpu_custom_call" | custom-call | flops 6000000000 | bytes 4194304 | tf_op jit(solution)/shard_map/attend_0/pallas_call | solution.py:224
  30.0 1.3 %collective-permute-start.9 = (bf16[16,8192]{1,0:T(8,128)(2,1)S(1)}, bf16[16,8192]{1,0:T(8,128)(2,1)S(1)}, u32[]{:S(2)}, u32[]{:S(2)}) collective-permute-start(bf16[16,8192]{1,0:T(8,128)(2,1)S(1)} %attend_0.1.refs_0_), channel_id=1, source_target_pairs={{10,0},{8,2},{11,4},{9,6},{26,16},{24,18},{27,20},{25,22}} | collective-permute-start | bytes 786440 | tf_op jit(solution)/shard_map/ppermute | solution.py:170
  31.4 0.0 collective-permute-done.6.queries
  31.4 1.5 %attend_1.1.refs_0_ = bf16[16,8192]{1,0:T(8,128)(2,1)S(1)} custom-call(s32[4]{0:T(128)S(1)} %copy-done.1, bf16[4,4,2,256,128]{4,3,2,1,0:T(8,128)(2,1)S(1)} %gather.1.pages_in, bf16[16,8192]{1,0:T(8,128)(2,1)S(1)} %collective-permute-done.6.queries, bf16[16,8192]{1,0:T(8,128)(2,1)S(1)} %attend_0.1.refs_0_), custom_call_target="tpu_custom_call" | custom-call | flops 6000000000 | bytes 4194304 | tf_op jit(solution)/shard_map/attend_1/pallas_call | solution.py:224
  32.9 1.3 %collective-permute-start.10 = (bf16[16,8192]{1,0:T(8,128)(2,1)S(1)}, bf16[16,8192]{1,0:T(8,128)(2,1)S(1)}, u32[]{:S(2)}, u32[]{:S(2)}) collective-permute-start(bf16[16,8192]{1,0:T(8,128)(2,1)S(1)} %attend_1.1.refs_0_), channel_id=1, source_target_pairs={{10,1},{8,3},{11,5},{9,7},{14,8},{12,10},{15,12},{13,14},{26,17},{... | collective-permute-start | bytes 786440 | tf_op jit(solution)/shard_map/ppermute | solution.py:170
  34.2 0.0 collective-permute-done.5.queries
  34.2 1.5 %attend_2.1.refs_0_ = bf16[16,8192]{1,0:T(8,128)(2,1)S(1)} custom-call(s32[4]{0:T(128)S(1)} %copy-done.1, bf16[4,4,2,256,128]{4,3,2,1,0:T(8,128)(2,1)S(1)} %gather.1.pages_in, bf16[16,8192]{1,0:T(8,128)(2,1)S(1)} %collective-permute-done.5.queries, bf16[16,8192]{1,0:T(8,128)(2,1)S(1)} %attend_1.1.refs_0_), custom_call_target="tpu_custom_call" | custom-call | flops 6000000000 | bytes 4194304 | tf_op jit(solution)/shard_map/attend_2/pallas_call | solution.py:224
  35.7 1.3 %collective-permute-start.11 = (bf16[16,8192]{1,0:T(8,128)(2,1)S(1)}, bf16[16,8192]{1,0:T(8,128)(2,1)S(1)}, u32[]{:S(2)}, u32[]{:S(2)}) collective-permute-start(bf16[16,8192]{1,0:T(8,128)(2,1)S(1)} %attend_2.1.refs_0_), channel_id=1, source_target_pairs={{8,0},{10,2},{9,4},{11,6},{12,8},{14,10},{13,12},{15,14},{24,16},{... | collective-permute-start | bytes 786440 | tf_op jit(solution)/shard_map/ppermute | solution.py:170
  37.0 0.0 collective-permute-done.4.queries
  37.1 1.9 %attend_3.1.refs_0_ = bf16[16,8192]{1,0:T(8,128)(2,1)S(1)} custom-call(s32[4]{0:T(128)S(1)} %copy-done.1, bf16[4,4,2,256,128]{4,3,2,1,0:T(8,128)(2,1)S(1)} %gather.1.pages_in, bf16[16,8192]{1,0:T(8,128)(2,1)S(1)} %collective-permute-done.4.queries, bf16[16,8192]{1,0:T(8,128)(2,1)S(1)} %attend_2.1.refs_0_), custom_call_target="tpu_custom_call" | custom-call | flops 6000000000 | bytes 4194304 | tf_op jit(solution)/shard_map/attend_3/pallas_call | solution.py:224
  39.0 1.9 %collective-permute-start.8 = (bf16[16,8192]{1,0:T(8,128)(2,1)S(1)}, bf16[16,8192]{1,0:T(8,128)(2,1)S(1)}, u32[]{:S(2)}, u32[]{:S(2)}) collective-permute-start(bf16[16,8192]{1,0:T(8,128)(2,1)S(1)} %attend_3.1.refs_0_), channel_id=1, source_target_pairs={{8,1},{10,3},{9,5},{11,7},{12,9},{14,11},{13,13},{15,15},{24,17},{... | collective-permute-start | bytes 786440 | tf_op jit(solution)/shard_map/ppermute | solution.py:170
  40.9 0.0 collective-permute-done.3.queries
  40.9 0.6 %attend_4.1 = bf16[16,8192]{1,0:T(8,128)(2,1)S(1)} custom-call(s32[4]{0:T(128)S(1)} %copy-done.1, bf16[4,4,2,256,128]{4,3,2,1,0:T(8,128)(2,1)S(1)} %gather.1.pages_in, bf16[16,8192]{1,0:T(8,128)(2,1)S(1)} %collective-permute-done.3.queries, bf16[16,8192]{1,0:T(8,128)(2,1)S(1)} %attend_3.1.refs_0_), custom_call_target="tpu_custom_call" | custom-call | flops 6000000000 | bytes 4194304 | tf_op jit(solution)/shard_map/attend_4/pallas_call | solution.py:224
  41.5 1.3 %collective-permute-start.7 = (bf16[16,8192]{1,0:T(8,128)(2,1)S(1)}, bf16[16,8192]{1,0:T(8,128)(2,1)S(1)}, u32[]{:S(2)}, u32[]{:S(2)}) collective-permute-start(bf16[16,8192]{1,0:T(8,128)(2,1)S(1)} %attend_4.1), channel_id=1, source_target_pairs={{14,9},{12,11},{15,13},{13,15},{30,25},{28,27},{31,29},{29,31}} | collective-permute-start | bytes 786440 | tf_op jit(solution)/shard_map/ppermute | solution.py:170
  42.8 0.0 collective-permute-done.11.refs_2_
  42.8 0.0 collective-permute-done.10.refs_1_
  42.8 0.0 collective-permute-done.9.refs_0_
  42.9 3.8 %collective-permute-done.8.refs_0_ = bf16[16,8192]{1,0:T(8,128)(2,1)S(1)} collective-permute-done((bf16[16,8192]{1,0:T(8,128)(2,1)S(1)}, bf16[16,8192]{1,0:T(8,128)(2,1)S(1)}, u32[]{:S(2)}, u32[]{:S(2)}) %collective-permute-start.8) | collective-permute-done | bytes 262176 | tf_op jit(solution)/shard_map/ppermute | solution.py:170
  46.7 0.7 %join.4.refs_1_ = bf16[16,16384]{1,0:T(8,128)(2,1)} custom-call(bf16[16,8192]{1,0:T(8,128)(2,1)S(1)} %collective-permute-done.8.refs_0_, bf16[16,16384]{1,0:T(8,128)(2,1)} %join.3.refs_1_), custom_call_target="tpu_custom_call", output_to_operand_aliasing={{}: (1, {})} | custom-call | tf_op jit(solution)/shard_map/join/pallas_call | solution.py:239
  47.4 4.0 %collective-permute-done.7.refs_0_ = bf16[16,8192]{1,0:T(8,128)(2,1)S(1)} collective-permute-done((bf16[16,8192]{1,0:T(8,128)(2,1)S(1)}, bf16[16,8192]{1,0:T(8,128)(2,1)S(1)}, u32[]{:S(2)}, u32[]{:S(2)}) %collective-permute-start.7) | collective-permute-done | bytes 262176 | tf_op jit(solution)/shard_map/ppermute | solution.py:170
  51.4 0.7 %join.5 = bf16[16,16384]{1,0:T(8,128)(2,1)} custom-call(bf16[16,8192]{1,0:T(8,128)(2,1)S(1)} %collective-permute-done.7.refs_0_, bf16[16,16384]{1,0:T(8,128)(2,1)} %join.4.refs_1_), custom_call_target="tpu_custom_call", output_to_operand_aliasing={{}: (1, {})} | custom-call | tf_op jit(solution)/shard_map/join/pallas_call | solution.py:239
  (2 shorter events, 0.0 us)
Async XLA Ops:
  0.0 26.3 %collective-permute-start = (bf16[2,512,512]{2,1,0:T(8,128)(2,1)}, bf16[2,512,512]{2,1,0:T(8,128)(2,1)S(1)}, u32[]{:S(2)}, u32[]{:S(2)}) collective-permute-start(bf16[2,512,512]{2,1,0:T(8,128)(2,1)} %own.1), channel_id=1, source_target_pairs={{9,12},{11,14},{12,9},{14,11},{25,28},{27,30},{28,25},{30,27}} | collective-permute-start | bytes 3145736 | tf_op jit(solution)/shard_map/ppermute | solution.py:170
  4.8 19.6 %collective-permute-start.2 = (bf16[16,8192]{1,0:T(8,128)(2,1)S(1)}, bf16[16,8192]{1,0:T(8,128)(2,1)S(1)}, u32[]{:S(2)}, u32[]{:S(2)}) collective-permute-start(bf16[16,8192]{1,0:T(8,128)(2,1)S(1)} %get-tuple-element.7), channel_id=1, source_target_pairs={{0,10},{2,8},{4,11},{6,9},{16,26},{18,24},{20,27},{22,25}} | collective-permute-start | bytes 786440 | tf_op jit(solution)/shard_map/ppermute | solution.py:170
  6.1 21.5 %collective-permute-start.1 = (bf16[2,512,512]{2,1,0:T(8,128)(2,1)}, bf16[2,512,512]{2,1,0:T(8,128)(2,1)S(1)}, u32[]{:S(2)}, u32[]{:S(2)}) collective-permute-start(bf16[2,512,512]{2,1,0:T(8,128)(2,1)} %own.1), channel_id=1, source_target_pairs={{8,9},{9,8},{10,11},{11,10},{12,13},{13,12},{14,15},{15,14},{24,25... | collective-permute-start | bytes 3145736 | tf_op jit(solution)/shard_map/ppermute | solution.py:170
  8.1 23.3 %collective-permute-start.6 = (bf16[16,8192]{1,0:T(8,128)(2,1)S(1)}, bf16[16,8192]{1,0:T(8,128)(2,1)S(1)}, u32[]{:S(2)}, u32[]{:S(2)}) collective-permute-start(bf16[16,8192]{1,0:T(8,128)(2,1)S(1)} %get-tuple-element.7), channel_id=1, source_target_pairs={{1,10},{3,8},{5,11},{7,9},{8,14},{10,12},{12,15},{14,13},{17,26},{... | collective-permute-start | bytes 786440 | tf_op jit(solution)/shard_map/ppermute | solution.py:170
  9.4 18.3 %copy-start = (bf16[2,512,512]{2,1,0:T(8,128)(2,1)S(1)}, bf16[2,512,512]{2,1,0:T(8,128)(2,1)}, u32[]{:S(2)}) copy-start(bf16[2,512,512]{2,1,0:T(8,128)(2,1)} %own.1) | copy-start | bytes 3145732
  9.4 18.3 %copy-start.1 = (s32[4]{0:T(128)S(1)}, s32[4]{0:T(128)}, u32[]{:S(2)}) copy-start(s32[4]{0:T(128)} %counts.11) | copy-start | bytes 52
  9.4 24.8 %collective-permute-start.5 = (bf16[16,8192]{1,0:T(8,128)(2,1)S(1)}, bf16[16,8192]{1,0:T(8,128)(2,1)S(1)}, u32[]{:S(2)}, u32[]{:S(2)}) collective-permute-start(bf16[16,8192]{1,0:T(8,128)(2,1)S(1)} %get-tuple-element.8), channel_id=1, source_target_pairs={{0,8},{2,10},{4,9},{6,11},{8,12},{10,14},{12,13},{14,15},{16,24},{... | collective-permute-start | bytes 786440 | tf_op jit(solution)/shard_map/ppermute | solution.py:170
  24.4 12.7 %collective-permute-start.4 = (bf16[16,8192]{1,0:T(8,128)(2,1)S(1)}, bf16[16,8192]{1,0:T(8,128)(2,1)S(1)}, u32[]{:S(2)}, u32[]{:S(2)}) collective-permute-start(bf16[16,8192]{1,0:T(8,128)(2,1)S(1)} %get-tuple-element.8), channel_id=1, source_target_pairs={{1,8},{3,10},{5,9},{7,11},{9,12},{11,14},{13,13},{15,15},{17,24},{... | collective-permute-start | bytes 786440 | tf_op jit(solution)/shard_map/ppermute | solution.py:170
  26.3 14.6 %collective-permute-start.3 = (bf16[16,8192]{1,0:T(8,128)(2,1)S(1)}, bf16[16,8192]{1,0:T(8,128)(2,1)S(1)}, u32[]{:S(2)}, u32[]{:S(2)}) collective-permute-start(bf16[16,8192]{1,0:T(8,128)(2,1)S(1)} %get-tuple-element.7), channel_id=1, source_target_pairs={{9,14},{11,12},{13,15},{15,13},{25,30},{27,28},{29,31},{31,29}} | collective-permute-start | bytes 786440 | tf_op jit(solution)/shard_map/ppermute | solution.py:170
  30.0 12.8 %collective-permute-start.9 = (bf16[16,8192]{1,0:T(8,128)(2,1)S(1)}, bf16[16,8192]{1,0:T(8,128)(2,1)S(1)}, u32[]{:S(2)}, u32[]{:S(2)}) collective-permute-start(bf16[16,8192]{1,0:T(8,128)(2,1)S(1)} %attend_0.1.refs_0_), channel_id=1, source_target_pairs={{10,0},{8,2},{11,4},{9,6},{26,16},{24,18},{27,20},{25,22}} | collective-permute-start | bytes 786440 | tf_op jit(solution)/shard_map/ppermute | solution.py:170
  32.9 9.9 %collective-permute-start.10 = (bf16[16,8192]{1,0:T(8,128)(2,1)S(1)}, bf16[16,8192]{1,0:T(8,128)(2,1)S(1)}, u32[]{:S(2)}, u32[]{:S(2)}) collective-permute-start(bf16[16,8192]{1,0:T(8,128)(2,1)S(1)} %attend_1.1.refs_0_), channel_id=1, source_target_pairs={{10,1},{8,3},{11,5},{9,7},{14,8},{12,10},{15,12},{13,14},{26,17},{... | collective-permute-start | bytes 786440 | tf_op jit(solution)/shard_map/ppermute | solution.py:170
  35.7 7.1 %collective-permute-start.11 = (bf16[16,8192]{1,0:T(8,128)(2,1)S(1)}, bf16[16,8192]{1,0:T(8,128)(2,1)S(1)}, u32[]{:S(2)}, u32[]{:S(2)}) collective-permute-start(bf16[16,8192]{1,0:T(8,128)(2,1)S(1)} %attend_2.1.refs_0_), channel_id=1, source_target_pairs={{8,0},{10,2},{9,4},{11,6},{12,8},{14,10},{13,12},{15,14},{24,16},{... | collective-permute-start | bytes 786440 | tf_op jit(solution)/shard_map/ppermute | solution.py:170
  39.0 7.7 %collective-permute-start.8 = (bf16[16,8192]{1,0:T(8,128)(2,1)S(1)}, bf16[16,8192]{1,0:T(8,128)(2,1)S(1)}, u32[]{:S(2)}, u32[]{:S(2)}) collective-permute-start(bf16[16,8192]{1,0:T(8,128)(2,1)S(1)} %attend_3.1.refs_0_), channel_id=1, source_target_pairs={{8,1},{10,3},{9,5},{11,7},{12,9},{14,11},{13,13},{15,15},{24,17},{... | collective-permute-start | bytes 786440 | tf_op jit(solution)/shard_map/ppermute | solution.py:170
  41.5 9.9 %collective-permute-start.7 = (bf16[16,8192]{1,0:T(8,128)(2,1)S(1)}, bf16[16,8192]{1,0:T(8,128)(2,1)S(1)}, u32[]{:S(2)}, u32[]{:S(2)}) collective-permute-start(bf16[16,8192]{1,0:T(8,128)(2,1)S(1)} %attend_4.1), channel_id=1, source_target_pairs={{14,9},{12,11},{15,13},{13,15},{30,25},{28,27},{31,29},{29,31}} | collective-permute-start | bytes 786440 | tf_op jit(solution)/shard_map/ppermute | solution.py:170

commit v3 on v2

--- a/solution.py
+++ b/solution.py
@@ -39,11 +39,11 @@
     ])
 
 
-def join_kernel(low_ctx, turns, *refs):
+def join_kernel(late_count, turns, *refs):
     out, sems = refs[-2:]
-    is_lower = lax.axis_index("ctx") < low_ctx
+    is_late = lax.axis_index("ctx") < late_count
     for piece, keys in zip(refs, turns):
-        for key, here in zip(keys, (is_lower, jnp.logical_not(is_lower))):
+        for key, here in zip(keys, (jnp.logical_not(is_late), is_late)):
             if key is not None:
                 @pl.when(here & (lax.axis_index("sub") == key[1]))
                 def _():
@@ -78,7 +78,7 @@
                             out[g, p, i] = ref[i, page_rows, g * HD:(g + 1) * HD]
 
 
-def attend_kernel(low_ctx, sub_count, turn, waits, counts, pages_in, queries, *refs):
+def attend_kernel(low_ctx, sub_count, late_count, turn, waits, counts, pages_in, queries, *refs):
     out = refs[waits]
     head = lax.axis_index("head")
     tokens, width = queries.shape
@@ -91,16 +91,17 @@
     def token_of(key):
         return ((head ^ key[0]) * sub_count + key[1]) * tokens
 
-    lower, upper = turn
-    if lower is None or upper is None:
-        first_token = token_of(lower or upper)
+    early, late = turn
+    is_late = request < late_count
+    if early is None or late is None:
+        first_token = token_of(early or late)
     else:
-        first_token = jnp.where(request < low_ctx, token_of(lower), token_of(upper))
-    works = (lax.axis_index("ctx") >= low_ctx)
-    if lower is None:
-        works = works & (request >= low_ctx)
-    if upper is None:
-        works = works & (request < low_ctx)
+        first_token = jnp.where(is_late, token_of(late), token_of(early))
+    works = lax.axis_index("ctx") >= low_ctx
+    if early is None:
+        works = works & is_late
+    if late is None:
+        works = works & jnp.logical_not(is_late)
 
     def attend(pages):
         token = lax.rem(lax.broadcasted_iota(jnp.int32, (rows, PAGE), 0), tokens)
@@ -182,14 +183,15 @@
         compiler_params=pltpu.CompilerParams(vmem_limit_bytes=2**20),
         name="split",
     )(hbm(queries))
-    lower = [(step, s) for step in heads[::-1] for s in range(sub_size)]
-    upper = [lower[0]] + lower[2:] + [lower[1]]
-    turns = list(zip(lower + [None], [None] + upper))
+    late_count = 1
+    early = [(step, s) for step in heads[::-1] for s in range(sub_size)]
+    late = [early[0]] + early[2:] + [early[1]]
+    turns = list(zip(early + [None], [None] + late))
 
     def routes_of(turn):
         return [
             ((r, h, key[1]), worker(r, h ^ key[0]))
-            for key, requests in zip(turn, (range(low_ctx), range(low_ctx, ctx_size))) if key is not None
+            for key, requests in zip(turn, (range(late_count, ctx_size), range(late_count))) if key is not None
             for r in requests for h in heads
         ]
 
@@ -222,7 +224,7 @@
     after = []
     for turn, arrived in zip(turns, q_in):
         out = pl.pallas_call(
-            functools.partial(attend_kernel, low_ctx, sub_size, turn, len(after)),
+            functools.partial(attend_kernel, low_ctx, sub_size, late_count, turn, len(after)),
             out_shape=q_piece,
             in_specs=[pl.BlockSpec(memory_space=pltpu.SMEM)] + [in_vmem] * 2 + [anywhere] * len(after),
             out_specs=in_vmem,
@@ -237,7 +239,7 @@
     for chosen in [range(len(turns) - 2)] + [[i] for i in range(len(turns) - 2, len(turns))]:
         joined = [
             pl.pallas_call(
-                functools.partial(join_kernel, low_ctx, [turns[i] for i in chosen]),
+                functools.partial(join_kernel, late_count, [turns[i] for i in chosen]),
                 out_shape=pltpu.HBM(queries.shape, queries.dtype),
                 in_specs=[anywhere] * (len(chosen) + len(joined)),
                 out_specs=anywhere,

time: 52.6 us -> 49.8 us (0.947)
  the two profiles are of different devices: /device:TPU:17 before, /device:TPU:1 now
where the time goes in v3:
time: 49.8 us; the launch traced here: 50.1 us
  starting transfers between devices  24.5 us (49%)
  waiting for transfers between devices  19 us (38%)
  Pallas kernels  6.09 us (12%)
    ppermute x12, starting transfers between devices, moved(): lax.ppermute(array, ('ctx', 'head', 'sub'), [(flat(a), flat(b)) for a, b...  24.5 us
    ppermute x12, waiting for transfers between devices, moved(): lax.ppermute(array, ('ctx', 'head', 'sub'), [(flat(a), flat(b)) for a, b...  19 us
    pallas_call x5, Pallas kernels, one_request_each(): pl.pallas_call(functools.partial(attend_kernel, low_ctx, sub_size, late_c...  3.02 us
    pallas_call x3, Pallas kernels, one_request_each(): pl.pallas_call(functools.partial(join_kernel, late_count, [turns[i] for i...  1.46 us
    pallas_call x1, Pallas kernels, one_request_each(): pl.pallas_call(split_kernel, out_shape=[q_piece] * head_count, in_specs=[...  1.06 us
  transfers between devices with their start and end apart: 12, of which 2 were waited for; matrix products, arithmetic and copies ran while one was open for 0% of the time, Pallas kernels for 11%

profile of v3, /device:TPU:1, one launch (start us, length us, event | category | flops | bytes accessed | tf_op | source)
XLA Modules:
  0.0 50.1 jit_solution(4454384057604516659)
XLA Ops:
  0.0 0.7 %collective-permute-start = (bf16[2,512,512]{2,1,0:T(8,128)(2,1)}, bf16[2,512,512]{2,1,0:T(8,128)(2,1)S(1)}, u32[]{:S(2)}, u32[]{:S(2)}) collective-permute-start(bf16[2,512,512]{2,1,0:T(8,128)(2,1)} %own.1), channel_id=1, source_target_pairs={{9,12},{11,14},{12,9},{14,11},{25,28},{27,30},{28,25},{30,27}} | collective-permute-start | bytes 3145736 | tf_op jit(solution)/shard_map/ppermute | solution.py:171
  0.7 1.1 %split.1 = (bf16[16,8192]{1,0:T(8,128)(2,1)S(1)}, bf16[16,8192]{1,0:T(8,128)(2,1)S(1)}) custom-call(bf16[16,16384]{1,0:T(8,128)(2,1)} %queries.1), custom_call_target="tpu_custom_call" | custom-call | tf_op jit(solution)/shard_map/split/pallas_call | solution.py:177
  1.8 0.7 %collective-permute-start.2 = (bf16[16,8192]{1,0:T(8,128)(2,1)S(1)}, bf16[16,8192]{1,0:T(8,128)(2,1)S(1)}, u32[]{:S(2)}, u32[]{:S(2)}) collective-permute-start(bf16[16,8192]{1,0:T(8,128)(2,1)S(1)} %get-tuple-element.7), channel_id=1, source_target_pairs={{4,11},{6,9},{8,14},{10,12},{12,15},{14,13},{20,27},{22,25},{24,30... | collective-permute-start | bytes 786440 | tf_op jit(solution)/shard_map/ppermute | solution.py:171
  2.5 0.7 %collective-permute-start.1 = (bf16[2,512,512]{2,1,0:T(8,128)(2,1)}, bf16[2,512,512]{2,1,0:T(8,128)(2,1)S(1)}, u32[]{:S(2)}, u32[]{:S(2)}) collective-permute-start(bf16[2,512,512]{2,1,0:T(8,128)(2,1)} %own.1), channel_id=1, source_target_pairs={{8,9},{9,8},{10,11},{11,10},{12,13},{13,12},{14,15},{15,14},{24,25... | collective-permute-start | bytes 3145736 | tf_op jit(solution)/shard_map/ppermute | solution.py:171
  3.2 0.7 %collective-permute-start.6 = (bf16[16,8192]{1,0:T(8,128)(2,1)S(1)}, bf16[16,8192]{1,0:T(8,128)(2,1)S(1)}, u32[]{:S(2)}, u32[]{:S(2)}) collective-permute-start(bf16[16,8192]{1,0:T(8,128)(2,1)S(1)} %get-tuple-element.7), channel_id=1, source_target_pairs={{5,11},{7,9},{9,14},{11,12},{13,15},{15,13},{0,10},{2,8},{21,27},{... | collective-permute-start | bytes 786440 | tf_op jit(solution)/shard_map/ppermute | solution.py:171
  3.9 0.0 copy-start
  3.9 0.0 copy-start.1
  3.9 0.8 %collective-permute-start.5 = (bf16[16,8192]{1,0:T(8,128)(2,1)S(1)}, bf16[16,8192]{1,0:T(8,128)(2,1)S(1)}, u32[]{:S(2)}, u32[]{:S(2)}) collective-permute-start(bf16[16,8192]{1,0:T(8,128)(2,1)S(1)} %get-tuple-element.8), channel_id=1, source_target_pairs={{4,9},{6,11},{8,12},{10,14},{12,13},{14,15},{0,8},{2,10},{20,25},{... | collective-permute-start | bytes 786440 | tf_op jit(solution)/shard_map/ppermute | solution.py:171
  4.7 0.0 collective-permute-done.2.refs_0_.queries
  4.7 15.0 %collective-permute-start.4 = (bf16[16,8192]{1,0:T(8,128)(2,1)S(1)}, bf16[16,8192]{1,0:T(8,128)(2,1)S(1)}, u32[]{:S(2)}, u32[]{:S(2)}) collective-permute-start(bf16[16,8192]{1,0:T(8,128)(2,1)S(1)} %get-tuple-element.8), channel_id=1, source_target_pairs={{5,9},{7,11},{9,12},{11,14},{13,13},{15,15},{1,8},{3,10},{21,25},{... | collective-permute-start | bytes 786440 | tf_op jit(solution)/shard_map/ppermute | solution.py:171
  19.8 0.0 collective-permute-done.refs_1_.far
  19.8 1.3 %collective-permute-start.3 = (bf16[16,8192]{1,0:T(8,128)(2,1)S(1)}, bf16[16,8192]{1,0:T(8,128)(2,1)S(1)}, u32[]{:S(2)}, u32[]{:S(2)}) collective-permute-start(bf16[16,8192]{1,0:T(8,128)(2,1)S(1)} %get-tuple-element.7), channel_id=1, source_target_pairs={{1,10},{3,8},{17,26},{19,24}} | collective-permute-start | bytes 786440 | tf_op jit(solution)/shard_map/ppermute | solution.py:171
  21.1 0.0 collective-permute-done.1.paired
  21.1 0.0 copy-done
  21.1 0.0 copy-done.1
  21.1 0.6 %gather.1.pages_in = bf16[4,4,2,256,128]{4,3,2,1,0:T(8,128)(2,1)S(1)} custom-call(s32[4]{0:T(128)S(1)} %copy-done.1, bf16[2,512,512]{2,1,0:T(8,128)(2,1)S(1)} %copy-done, bf16[2,512,512]{2,1,0:T(8,128)(2,1)S(1)} %collective-permute-done.refs_1_.far, bf16[2,512,512]{2,1,0:T(8,128)(2,1)S(1)} %collective-permute-done.1.paired, f32[8,128]{1,0:T(8,128)S(1)} %first_here.1.after), custom_call_target="tpu_custom_call" | custom-call | tf_op jit(solution)/shard_map/gather/pallas_call | solution.py:214
  21.7 0.6 %attend_0.1.refs_0_ = bf16[16,8192]{1,0:T(8,128)(2,1)S(1)} custom-call(s32[4]{0:T(128)S(1)} %copy-done.1, bf16[4,4,2,256,128]{4,3,2,1,0:T(8,128)(2,1)S(1)} %gather.1.pages_in, bf16[16,8192]{1,0:T(8,128)(2,1)S(1)} %collective-permute-done.2.refs_0_.queries), custom_call_target="tpu_custom_call" | custom-call | flops 6000000000 | bytes 4194304 | tf_op jit(solution)/shard_map/attend_0/pallas_call | solution.py:226
  22.3 0.7 %collective-permute-start.9 = (bf16[16,8192]{1,0:T(8,128)(2,1)S(1)}, bf16[16,8192]{1,0:T(8,128)(2,1)S(1)}, u32[]{:S(2)}, u32[]{:S(2)}) collective-permute-start(bf16[16,8192]{1,0:T(8,128)(2,1)S(1)} %attend_0.1.refs_0_), channel_id=1, source_target_pairs={{11,4},{9,6},{14,8},{12,10},{15,12},{13,14},{27,20},{25,22},{30,24... | collective-permute-start | bytes 786440 | tf_op jit(solution)/shard_map/ppermute | solution.py:171
  22.9 0.0 collective-permute-done.6.queries
  23.0 0.6 %attend_1.1.refs_0_ = bf16[16,8192]{1,0:T(8,128)(2,1)S(1)} custom-call(s32[4]{0:T(128)S(1)} %copy-done.1, bf16[4,4,2,256,128]{4,3,2,1,0:T(8,128)(2,1)S(1)} %gather.1.pages_in, bf16[16,8192]{1,0:T(8,128)(2,1)S(1)} %collective-permute-done.6.queries, bf16[16,8192]{1,0:T(8,128)(2,1)S(1)} %attend_0.1.refs_0_), custom_call_target="tpu_custom_call" | custom-call | flops 6000000000 | bytes 4194304 | tf_op jit(solution)/shard_map/attend_1/pallas_call | solution.py:226
  23.5 0.7 %collective-permute-start.10 = (bf16[16,8192]{1,0:T(8,128)(2,1)S(1)}, bf16[16,8192]{1,0:T(8,128)(2,1)S(1)}, u32[]{:S(2)}, u32[]{:S(2)}) collective-permute-start(bf16[16,8192]{1,0:T(8,128)(2,1)S(1)} %attend_1.1.refs_0_), channel_id=1, source_target_pairs={{11,5},{9,7},{14,9},{12,11},{15,13},{13,15},{10,0},{8,2},{27,21},{... | collective-permute-start | bytes 786440 | tf_op jit(solution)/shard_map/ppermute | solution.py:171
  24.2 0.0 collective-permute-done.5.queries
  24.2 0.6 %attend_2.1.refs_0_ = bf16[16,8192]{1,0:T(8,128)(2,1)S(1)} custom-call(s32[4]{0:T(128)S(1)} %copy-done.1, bf16[4,4,2,256,128]{4,3,2,1,0:T(8,128)(2,1)S(1)} %gather.1.pages_in, bf16[16,8192]{1,0:T(8,128)(2,1)S(1)} %collective-permute-done.5.queries, bf16[16,8192]{1,0:T(8,128)(2,1)S(1)} %attend_1.1.refs_0_), custom_call_target="tpu_custom_call" | custom-call | flops 6000000000 | bytes 4194304 | tf_op jit(solution)/shard_map/attend_2/pallas_call | solution.py:226
  24.8 0.7 %collective-permute-start.11 = (bf16[16,8192]{1,0:T(8,128)(2,1)S(1)}, bf16[16,8192]{1,0:T(8,128)(2,1)S(1)}, u32[]{:S(2)}, u32[]{:S(2)}) collective-permute-start(bf16[16,8192]{1,0:T(8,128)(2,1)S(1)} %attend_2.1.refs_0_), channel_id=1, source_target_pairs={{9,4},{11,6},{12,8},{14,10},{13,12},{15,14},{8,0},{10,2},{25,20},{... | collective-permute-start | bytes 786440 | tf_op jit(solution)/shard_map/ppermute | solution.py:171
  25.5 0.0 collective-permute-done.4.queries
  25.5 0.8 %attend_3.1.refs_0_ = bf16[16,8192]{1,0:T(8,128)(2,1)S(1)} custom-call(s32[4]{0:T(128)S(1)} %copy-done.1, bf16[4,4,2,256,128]{4,3,2,1,0:T(8,128)(2,1)S(1)} %gather.1.pages_in, bf16[16,8192]{1,0:T(8,128)(2,1)S(1)} %collective-permute-done.4.queries, bf16[16,8192]{1,0:T(8,128)(2,1)S(1)} %attend_2.1.refs_0_), custom_call_target="tpu_custom_call" | custom-call | flops 6000000000 | bytes 4194304 | tf_op jit(solution)/shard_map/attend_3/pallas_call | solution.py:226
  26.3 1.3 %collective-permute-start.8 = (bf16[16,8192]{1,0:T(8,128)(2,1)S(1)}, bf16[16,8192]{1,0:T(8,128)(2,1)S(1)}, u32[]{:S(2)}, u32[]{:S(2)}) collective-permute-start(bf16[16,8192]{1,0:T(8,128)(2,1)S(1)} %attend_3.1.refs_0_), channel_id=1, source_target_pairs={{9,5},{11,7},{12,9},{14,11},{13,13},{15,15},{8,1},{10,3},{25,21},{... | collective-permute-start | bytes 786440 | tf_op jit(solution)/shard_map/ppermute | solution.py:171
  27.6 0.0 collective-permute-done.3.queries
  27.6 0.6 %attend_4.1 = bf16[16,8192]{1,0:T(8,128)(2,1)S(1)} custom-call(s32[4]{0:T(128)S(1)} %copy-done.1, bf16[4,4,2,256,128]{4,3,2,1,0:T(8,128)(2,1)S(1)} %gather.1.pages_in, bf16[16,8192]{1,0:T(8,128)(2,1)S(1)} %collective-permute-done.3.queries, bf16[16,8192]{1,0:T(8,128)(2,1)S(1)} %attend_3.1.refs_0_), custom_call_target="tpu_custom_call" | custom-call | flops 6000000000 | bytes 4194304 | tf_op jit(solution)/shard_map/attend_4/pallas_call | solution.py:226
  28.1 1.3 %collective-permute-start.7 = (bf16[16,8192]{1,0:T(8,128)(2,1)S(1)}, bf16[16,8192]{1,0:T(8,128)(2,1)S(1)}, u32[]{:S(2)}, u32[]{:S(2)}) collective-permute-start(bf16[16,8192]{1,0:T(8,128)(2,1)S(1)} %attend_4.1), channel_id=1, source_target_pairs={{10,1},{8,3},{26,17},{24,19}} | collective-permute-start | bytes 786440 | tf_op jit(solution)/shard_map/ppermute | solution.py:171
  29.4 0.0 collective-permute-done.11.refs_2_
  29.5 0.0 collective-permute-done.10.refs_1_
  29.5 0.0 collective-permute-done.9.refs_0_
  29.5 12.2 %collective-permute-done.8.refs_0_ = bf16[16,8192]{1,0:T(8,128)(2,1)S(1)} collective-permute-done((bf16[16,8192]{1,0:T(8,128)(2,1)S(1)}, bf16[16,8192]{1,0:T(8,128)(2,1)S(1)}, u32[]{:S(2)}, u32[]{:S(2)}) %collective-permute-start.8) | collective-permute-done | bytes 262176 | tf_op jit(solution)/shard_map/ppermute | solution.py:171
  41.7 0.7 %join.4.refs_1_ = bf16[16,16384]{1,0:T(8,128)(2,1)} custom-call(bf16[16,8192]{1,0:T(8,128)(2,1)S(1)} %collective-permute-done.8.refs_0_, bf16[16,16384]{1,0:T(8,128)(2,1)} %join.3.refs_1_), custom_call_target="tpu_custom_call", output_to_operand_aliasing={{}: (1, {})} | custom-call | tf_op jit(solution)/shard_map/join/pallas_call | solution.py:241
  42.4 6.8 %collective-permute-done.7.refs_0_ = bf16[16,8192]{1,0:T(8,128)(2,1)S(1)} collective-permute-done((bf16[16,8192]{1,0:T(8,128)(2,1)S(1)}, bf16[16,8192]{1,0:T(8,128)(2,1)S(1)}, u32[]{:S(2)}, u32[]{:S(2)}) %collective-permute-start.7) | collective-permute-done | bytes 262176 | tf_op jit(solution)/shard_map/ppermute | solution.py:171
  49.2 0.7 %join.5 = bf16[16,16384]{1,0:T(8,128)(2,1)} custom-call(bf16[16,8192]{1,0:T(8,128)(2,1)S(1)} %collective-permute-done.7.refs_0_, bf16[16,16384]{1,0:T(8,128)(2,1)} %join.4.refs_1_), custom_call_target="tpu_custom_call", output_to_operand_aliasing={{}: (1, {})} | custom-call | tf_op jit(solution)/shard_map/join/pallas_call | solution.py:241
  (2 shorter events, 0.0 us)
Async XLA Ops:
  0.0 19.8 %collective-permute-start = (bf16[2,512,512]{2,1,0:T(8,128)(2,1)}, bf16[2,512,512]{2,1,0:T(8,128)(2,1)S(1)}, u32[]{:S(2)}, u32[]{:S(2)}) collective-permute-start(bf16[2,512,512]{2,1,0:T(8,128)(2,1)} %own.1), channel_id=1, source_target_pairs={{9,12},{11,14},{12,9},{14,11},{25,28},{27,30},{28,25},{30,27}} | collective-permute-start | bytes 3145736 | tf_op jit(solution)/shard_map/ppermute | solution.py:171
  1.8 3.0 %collective-permute-start.2 = (bf16[16,8192]{1,0:T(8,128)(2,1)S(1)}, bf16[16,8192]{1,0:T(8,128)(2,1)S(1)}, u32[]{:S(2)}, u32[]{:S(2)}) collective-permute-start(bf16[16,8192]{1,0:T(8,128)(2,1)S(1)} %get-tuple-element.7), channel_id=1, source_target_pairs={{4,11},{6,9},{8,14},{10,12},{12,15},{14,13},{20,27},{22,25},{24,30... | collective-permute-start | bytes 786440 | tf_op jit(solution)/shard_map/ppermute | solution.py:171
  2.5 18.6 %collective-permute-start.1 = (bf16[2,512,512]{2,1,0:T(8,128)(2,1)}, bf16[2,512,512]{2,1,0:T(8,128)(2,1)S(1)}, u32[]{:S(2)}, u32[]{:S(2)}) collective-permute-start(bf16[2,512,512]{2,1,0:T(8,128)(2,1)} %own.1), channel_id=1, source_target_pairs={{8,9},{9,8},{10,11},{11,10},{12,13},{13,12},{14,15},{15,14},{24,25... | collective-permute-start | bytes 3145736 | tf_op jit(solution)/shard_map/ppermute | solution.py:171
  3.2 19.7 %collective-permute-start.6 = (bf16[16,8192]{1,0:T(8,128)(2,1)S(1)}, bf16[16,8192]{1,0:T(8,128)(2,1)S(1)}, u32[]{:S(2)}, u32[]{:S(2)}) collective-permute-start(bf16[16,8192]{1,0:T(8,128)(2,1)S(1)} %get-tuple-element.7), channel_id=1, source_target_pairs={{5,11},{7,9},{9,14},{11,12},{13,15},{15,13},{0,10},{2,8},{21,27},{... | collective-permute-start | bytes 786440 | tf_op jit(solution)/shard_map/ppermute | solution.py:171
  3.9 17.2 %copy-start = (bf16[2,512,512]{2,1,0:T(8,128)(2,1)S(1)}, bf16[2,512,512]{2,1,0:T(8,128)(2,1)}, u32[]{:S(2)}) copy-start(bf16[2,512,512]{2,1,0:T(8,128)(2,1)} %own.1) | copy-start | bytes 3145732
  3.9 17.2 %copy-start.1 = (s32[4]{0:T(128)S(1)}, s32[4]{0:T(128)}, u32[]{:S(2)}) copy-start(s32[4]{0:T(128)} %counts.11) | copy-start | bytes 52
  3.9 20.3 %collective-permute-start.5 = (bf16[16,8192]{1,0:T(8,128)(2,1)S(1)}, bf16[16,8192]{1,0:T(8,128)(2,1)S(1)}, u32[]{:S(2)}, u32[]{:S(2)}) collective-permute-start(bf16[16,8192]{1,0:T(8,128)(2,1)S(1)} %get-tuple-element.8), channel_id=1, source_target_pairs={{4,9},{6,11},{8,12},{10,14},{12,13},{14,15},{0,8},{2,10},{20,25},{... | collective-permute-start | bytes 786440 | tf_op jit(solution)/shard_map/ppermute | solution.py:171
  4.7 20.7 %collective-permute-start.4 = (bf16[16,8192]{1,0:T(8,128)(2,1)S(1)}, bf16[16,8192]{1,0:T(8,128)(2,1)S(1)}, u32[]{:S(2)}, u32[]{:S(2)}) collective-permute-start(bf16[16,8192]{1,0:T(8,128)(2,1)S(1)} %get-tuple-element.8), channel_id=1, source_target_pairs={{5,9},{7,11},{9,12},{11,14},{13,13},{15,15},{1,8},{3,10},{21,25},{... | collective-permute-start | bytes 786440 | tf_op jit(solution)/shard_map/ppermute | solution.py:171
  19.8 7.8 %collective-permute-start.3 = (bf16[16,8192]{1,0:T(8,128)(2,1)S(1)}, bf16[16,8192]{1,0:T(8,128)(2,1)S(1)}, u32[]{:S(2)}, u32[]{:S(2)}) collective-permute-start(bf16[16,8192]{1,0:T(8,128)(2,1)S(1)} %get-tuple-element.7), channel_id=1, source_target_pairs={{1,10},{3,8},{17,26},{19,24}} | collective-permute-start | bytes 786440 | tf_op jit(solution)/shard_map/ppermute | solution.py:171
  22.3 7.2 %collective-permute-start.9 = (bf16[16,8192]{1,0:T(8,128)(2,1)S(1)}, bf16[16,8192]{1,0:T(8,128)(2,1)S(1)}, u32[]{:S(2)}, u32[]{:S(2)}) collective-permute-start(bf16[16,8192]{1,0:T(8,128)(2,1)S(1)} %attend_0.1.refs_0_), channel_id=1, source_target_pairs={{11,4},{9,6},{14,8},{12,10},{15,12},{13,14},{27,20},{25,22},{30,24... | collective-permute-start | bytes 786440 | tf_op jit(solution)/shard_map/ppermute | solution.py:171
  23.5 5.9 %collective-permute-start.10 = (bf16[16,8192]{1,0:T(8,128)(2,1)S(1)}, bf16[16,8192]{1,0:T(8,128)(2,1)S(1)}, u32[]{:S(2)}, u32[]{:S(2)}) collective-permute-start(bf16[16,8192]{1,0:T(8,128)(2,1)S(1)} %attend_1.1.refs_0_), channel_id=1, source_target_pairs={{11,5},{9,7},{14,9},{12,11},{15,13},{13,15},{10,0},{8,2},{27,21},{... | collective-permute-start | bytes 786440 | tf_op jit(solution)/shard_map/ppermute | solution.py:171
  24.8 4.7 %collective-permute-start.11 = (bf16[16,8192]{1,0:T(8,128)(2,1)S(1)}, bf16[16,8192]{1,0:T(8,128)(2,1)S(1)}, u32[]{:S(2)}, u32[]{:S(2)}) collective-permute-start(bf16[16,8192]{1,0:T(8,128)(2,1)S(1)} %attend_2.1.refs_0_), channel_id=1, source_target_pairs={{9,4},{11,6},{12,8},{14,10},{13,12},{15,14},{8,0},{10,2},{25,20},{... | collective-permute-start | bytes 786440 | tf_op jit(solution)/shard_map/ppermute | solution.py:171
  26.3 15.4 %collective-permute-start.8 = (bf16[16,8192]{1,0:T(8,128)(2,1)S(1)}, bf16[16,8192]{1,0:T(8,128)(2,1)S(1)}, u32[]{:S(2)}, u32[]{:S(2)}) collective-permute-start(bf16[16,8192]{1,0:T(8,128)(2,1)S(1)} %attend_3.1.refs_0_), channel_id=1, source_target_pairs={{9,5},{11,7},{12,9},{14,11},{13,13},{15,15},{8,1},{10,3},{25,21},{... | collective-permute-start | bytes 786440 | tf_op jit(solution)/shard_map/ppermute | solution.py:171
  28.1 21.1 %collective-permute-start.7 = (bf16[16,8192]{1,0:T(8,128)(2,1)S(1)}, bf16[16,8192]{1,0:T(8,128)(2,1)S(1)}, u32[]{:S(2)}, u32[]{:S(2)}) collective-permute-start(bf16[16,8192]{1,0:T(8,128)(2,1)S(1)} %attend_4.1), channel_id=1, source_target_pairs={{10,1},{8,3},{26,17},{24,19}} | collective-permute-start | bytes 786440 | tf_op jit(solution)/shard_map/ppermute | solution.py:171

commit v4 on v0

--- a/solution.py
+++ b/solution.py
@@ -47,25 +47,33 @@
             run([pltpu.make_async_copy(refs[i], out.at[:, head_part(step, refs[i].shape[1])], sems.at[0])])
 
 
-def own_pair_of(low_ctx, sub_count):
-    return (lax.axis_index("ctx") - low_ctx) * sub_count + lax.axis_index("sub")
+def worker_places(low_ctx):
+    return (low_ctx, 0), (low_ctx, 1), (low_ctx + 1, 1), (low_ctx + 1, 0)
+
+
+def own_request(low_ctx):
+    ctx, sub = lax.axis_index("ctx"), lax.axis_index("sub")
+    found = jnp.int32(-1)
+    for request, place in enumerate(worker_places(low_ctx)):
+        found = jnp.where((ctx == place[0]) & (sub == place[1]), request, found)
+    return found
 
 
 def gather_kernel(low_ctx, sub_count, counts, own, far, paired, after, out):
     local_kv, most_pages = out.shape[:2]
-    own_pair = own_pair_of(low_ctx, sub_count)
-    sub = lax.axis_index("sub")
-
-    @pl.when(lax.axis_index("ctx") >= low_ctx)
+    request = own_request(low_ctx)
+    home_pair = (lax.axis_index("ctx") - low_ctx) * sub_count + lax.axis_index("sub")
+
+    @pl.when(request >= 0)
     def _():
         start = jnp.int32(0)
         for r in range(REQS):
-            start = start + jnp.where(r < own_pair, counts[r], 0)
-        count = counts[own_pair]
+            start = start + jnp.where(r < request, counts[r], 0)
+        count = counts[request]
         for p in range(most_pages):
             page = start + p
-            apart = page // 2 - own_pair
-            which = jnp.where(apart == 0, 0, jnp.where(apart == 1 - 2 * sub, 1, 2))
+            pair = page // 2
+            which = jnp.where(pair == home_pair, 0, jnp.where(pair == (home_pair ^ 1), 1, 2))
             page_rows = pl.ds(pl.multiple_of(lax.rem(page, 2) * PAGE, PAGE), PAGE)
             for n, ref in enumerate((own, paired, far)):
                 @pl.when((p < count) & (which == n))
@@ -120,9 +128,11 @@
             )
             scores = later
 
-    @pl.when(lax.axis_index("ctx") >= low_ctx)
+    request = own_request(low_ctx)
+
+    @pl.when(request >= 0)
     def _():
-        count = counts[own_pair_of(low_ctx, sub_count)]
+        count = counts[request]
         for pages in [*range(1, most_pages - REQS + 3), most_pages]:
             @pl.when(count == pages)
             def _():
@@ -153,7 +163,8 @@
         return lax.ppermute(array, ("ctx", "head", "sub"), [(flat(a), flat(b)) for a, b in routes])
 
     def worker(request, head):
-        return low_ctx + request // sub_size, head, request % sub_size
+        ctx, sub = worker_places(low_ctx)[request]
+        return ctx, head, sub
 
     heads = range(head_count)
     q_out = pl.pallas_call(
@@ -172,8 +183,8 @@
     q_in = {key: moved(q_out[key[0]], pairs) for key, pairs in routes.items()}
     first = list(routes)[0]
 
-    middle = [(low_ctx, sub_size - 1), (low_ctx + 1, 0)]
-    far = moved(kv_cache, [((a[0], h, a[1]), (b[0], h, b[1])) for a, b in (middle, middle[::-1]) for h in heads])
+    sends = [((low_ctx, sub_size - 1), worker_places(low_ctx)[2]), ((low_ctx + 1, 0), worker_places(low_ctx)[1])]
+    far = moved(kv_cache, [((a[0], h, a[1]), (b[0], h, b[1])) for a, b in sends for h in heads])
     paired = moved(
         kv_cache, [((c, h, s), (c, h, 1 - s)) for c in range(low_ctx, ctx_size) for h in heads for s in range(sub_size)]
     )

time: 47.7 us -> 50.4 us (1.057)
  the two profiles are of different devices: /device:TPU:13 before, /device:TPU:15 now
where the time goes in v4:
time: 50.4 us; the launch traced here: 50.2 us
  starting transfers between devices  30.6 us (61%)
  waiting for transfers between devices  13.6 us (27%)
  Pallas kernels  5.54 us (11%)
    ppermute x10, starting transfers between devices, moved(): lax.ppermute(array, ('ctx', 'head', 'sub'), [(flat(a), flat(b)) for a, b...  30.6 us
    ppermute x10, waiting for transfers between devices, moved(): lax.ppermute(array, ('ctx', 'head', 'sub'), [(flat(a), flat(b)) for a, b...  13.6 us
    pallas_call x4, Pallas kernels, one_request_each(): pl.pallas_call(functools.partial(attend_kernel, low_ctx, sub_size, step,...  2.47 us
    pallas_call x3, Pallas kernels, one_request_each(): pl.pallas_call(functools.partial(join_kernel, keys), out_shape=pltpu.HBM(...  1.45 us
    pallas_call x1, Pallas kernels, one_request_each(): pl.pallas_call(split_kernel, out_shape=[q_piece] * head_count, in_specs=[...  1.06 us
  transfers between devices with their start and end apart: 10, of which 2 were waited for; matrix products, arithmetic and copies ran while one was open for 0% of the time, Pallas kernels for 10%

profile of v4, /device:TPU:15, one launch (start us, length us, event | category | flops | bytes accessed | tf_op | source)
XLA Modules:
  0.0 50.2 jit_solution(10866939720906370058)
XLA Ops:
  0.0 0.7 %collective-permute-start = (bf16[2,512,512]{2,1,0:T(8,128)(2,1)}, bf16[2,512,512]{2,1,0:T(8,128)(2,1)S(1)}, u32[]{:S(2)}, u32[]{:S(2)}) collective-permute-start(bf16[2,512,512]{2,1,0:T(8,128)(2,1)} %own.1), channel_id=1, source_target_pairs={{9,13},{11,15},{12,9},{14,11},{25,29},{27,31},{28,25},{30,27}} | collective-permute-start | bytes 3145736 | tf_op jit(solution)/shard_map/ppermute | solution.py:163
  0.7 1.1 %split.1 = (bf16[16,8192]{1,0:T(8,128)(2,1)S(1)}, bf16[16,8192]{1,0:T(8,128)(2,1)S(1)}) custom-call(bf16[16,16384]{1,0:T(8,128)(2,1)} %queries.1), custom_call_target="tpu_custom_call" | custom-call | tf_op jit(solution)/shard_map/split/pallas_call | solution.py:170
  1.8 0.7 %collective-permute-start.2 = (bf16[16,8192]{1,0:T(8,128)(2,1)S(1)}, bf16[16,8192]{1,0:T(8,128)(2,1)S(1)}, u32[]{:S(2)}, u32[]{:S(2)}) collective-permute-start(bf16[16,8192]{1,0:T(8,128)(2,1)S(1)} %get-tuple-element.7), channel_id=1, source_target_pairs={{0,10},{2,8},{4,11},{6,9},{8,15},{10,13},{12,14},{14,12},{16,26},{... | collective-permute-start | bytes 786440 | tf_op jit(solution)/shard_map/ppermute | solution.py:163
  2.5 0.7 %collective-permute-start.1 = (bf16[2,512,512]{2,1,0:T(8,128)(2,1)}, bf16[2,512,512]{2,1,0:T(8,128)(2,1)S(1)}, u32[]{:S(2)}, u32[]{:S(2)}) collective-permute-start(bf16[2,512,512]{2,1,0:T(8,128)(2,1)} %own.1), channel_id=1, source_target_pairs={{8,9},{9,8},{10,11},{11,10},{12,13},{13,12},{14,15},{15,14},{24,25... | collective-permute-start | bytes 3145736 | tf_op jit(solution)/shard_map/ppermute | solution.py:163
  3.2 8.8 %collective-permute-start.5 = (bf16[16,8192]{1,0:T(8,128)(2,1)S(1)}, bf16[16,8192]{1,0:T(8,128)(2,1)S(1)}, u32[]{:S(2)}, u32[]{:S(2)}) collective-permute-start(bf16[16,8192]{1,0:T(8,128)(2,1)S(1)} %get-tuple-element.7), channel_id=1, source_target_pairs={{1,10},{3,8},{5,11},{7,9},{9,15},{11,13},{13,14},{15,12},{17,26},{... | collective-permute-start | bytes 786440 | tf_op jit(solution)/shard_map/ppermute | solution.py:163
  12.0 0.0 copy-start
  12.0 0.0 copy-start.1
  12.0 0.8 %collective-permute-start.4 = (bf16[16,8192]{1,0:T(8,128)(2,1)S(1)}, bf16[16,8192]{1,0:T(8,128)(2,1)S(1)}, u32[]{:S(2)}, u32[]{:S(2)}) collective-permute-start(bf16[16,8192]{1,0:T(8,128)(2,1)S(1)} %get-tuple-element.8), channel_id=1, source_target_pairs={{0,8},{2,10},{4,9},{6,11},{8,13},{10,15},{12,12},{14,14},{16,24},{... | collective-permute-start | bytes 786440 | tf_op jit(solution)/shard_map/ppermute | solution.py:163
  12.8 0.0 collective-permute-done.2.refs_0_.queries
  12.9 14.9 %collective-permute-start.3 = (bf16[16,8192]{1,0:T(8,128)(2,1)S(1)}, bf16[16,8192]{1,0:T(8,128)(2,1)S(1)}, u32[]{:S(2)}, u32[]{:S(2)}) collective-permute-start(bf16[16,8192]{1,0:T(8,128)(2,1)S(1)} %get-tuple-element.8), channel_id=1, source_target_pairs={{1,8},{3,10},{5,9},{7,11},{9,13},{11,15},{13,12},{15,14},{17,24},{... | collective-permute-start | bytes 786440 | tf_op jit(solution)/shard_map/ppermute | solution.py:163
  27.8 0.0 collective-permute-done.refs_1_.far
  27.8 0.0 collective-permute-done.1.paired
  27.8 0.0 copy-done
  27.8 0.0 copy-done.1
  27.9 0.6 %gather.1.pages_in = bf16[4,4,2,256,128]{4,3,2,1,0:T(8,128)(2,1)S(1)} custom-call(s32[4]{0:T(128)S(1)} %copy-done.1, bf16[2,512,512]{2,1,0:T(8,128)(2,1)S(1)} %copy-done, bf16[2,512,512]{2,1,0:T(8,128)(2,1)S(1)} %collective-permute-done.refs_1_.far, bf16[2,512,512]{2,1,0:T(8,128)(2,1)S(1)} %collective-permute-done.1.paired, f32[8,128]{1,0:T(8,128)S(1)} %first_here.1.after), custom_call_target="tpu_custom_call" | custom-call | tf_op jit(solution)/shard_map/gather/pallas_call | solution.py:200
  28.4 0.6 %attend_10.1.refs_0_ = bf16[16,8192]{1,0:T(8,128)(2,1)S(1)} custom-call(s32[4]{0:T(128)S(1)} %copy-done.1, bf16[4,4,2,256,128]{4,3,2,1,0:T(8,128)(2,1)S(1)} %gather.1.pages_in, bf16[16,8192]{1,0:T(8,128)(2,1)S(1)} %collective-permute-done.2.refs_0_.queries), custom_call_target="tpu_custom_call" | custom-call | flops 6000000000 | bytes 4194304 | tf_op jit(solution)/shard_map/attend_10/pallas_call | solution.py:212
  29.0 0.7 %collective-permute-start.8 = (bf16[16,8192]{1,0:T(8,128)(2,1)S(1)}, bf16[16,8192]{1,0:T(8,128)(2,1)S(1)}, u32[]{:S(2)}, u32[]{:S(2)}) collective-permute-start(bf16[16,8192]{1,0:T(8,128)(2,1)S(1)} %attend_10.1.refs_0_), channel_id=1, source_target_pairs={{10,0},{8,2},{11,4},{9,6},{15,8},{13,10},{14,12},{12,14},{26,16},{... | collective-permute-start | bytes 786440 | tf_op jit(solution)/shard_map/ppermute | solution.py:163
  29.7 0.0 collective-permute-done.5.queries
  29.7 0.6 %attend_11.1.refs_0_ = bf16[16,8192]{1,0:T(8,128)(2,1)S(1)} custom-call(s32[4]{0:T(128)S(1)} %copy-done.1, bf16[4,4,2,256,128]{4,3,2,1,0:T(8,128)(2,1)S(1)} %gather.1.pages_in, bf16[16,8192]{1,0:T(8,128)(2,1)S(1)} %collective-permute-done.5.queries, bf16[16,8192]{1,0:T(8,128)(2,1)S(1)} %attend_10.1.refs_0_), custom_call_target="tpu_custom_call" | custom-call | flops 6000000000 | bytes 4194304 | tf_op jit(solution)/shard_map/attend_11/pallas_call | solution.py:212
  30.3 1.3 %collective-permute-start.9 = (bf16[16,8192]{1,0:T(8,128)(2,1)S(1)}, bf16[16,8192]{1,0:T(8,128)(2,1)S(1)}, u32[]{:S(2)}, u32[]{:S(2)}) collective-permute-start(bf16[16,8192]{1,0:T(8,128)(2,1)S(1)} %attend_11.1.refs_0_), channel_id=1, source_target_pairs={{10,1},{8,3},{11,5},{9,7},{15,9},{13,11},{14,13},{12,15},{26,17},{... | collective-permute-start | bytes 786440 | tf_op jit(solution)/shard_map/ppermute | solution.py:163
  31.6 0.0 collective-permute-done.4.queries
  31.6 0.6 %attend_00.1.refs_0_ = bf16[16,8192]{1,0:T(8,128)(2,1)S(1)} custom-call(s32[4]{0:T(128)S(1)} %copy-done.1, bf16[4,4,2,256,128]{4,3,2,1,0:T(8,128)(2,1)S(1)} %gather.1.pages_in, bf16[16,8192]{1,0:T(8,128)(2,1)S(1)} %collective-permute-done.4.queries, bf16[16,8192]{1,0:T(8,128)(2,1)S(1)} %attend_11.1.refs_0_), custom_call_target="tpu_custom_call" | custom-call | flops 6000000000 | bytes 4194304 | tf_op jit(solution)/shard_map/attend_00/pallas_call | solution.py:212
  32.1 0.7 %collective-permute-start.7 = (bf16[16,8192]{1,0:T(8,128)(2,1)S(1)}, bf16[16,8192]{1,0:T(8,128)(2,1)S(1)}, u32[]{:S(2)}, u32[]{:S(2)}) collective-permute-start(bf16[16,8192]{1,0:T(8,128)(2,1)S(1)} %attend_00.1.refs_0_), channel_id=1, source_target_pairs={{8,0},{10,2},{9,4},{11,6},{13,8},{15,10},{12,12},{14,14},{24,16},{... | collective-permute-start | bytes 786440 | tf_op jit(solution)/shard_map/ppermute | solution.py:163
  32.8 0.0 collective-permute-done.3.queries
  32.8 0.8 %attend_01.1 = bf16[16,8192]{1,0:T(8,128)(2,1)S(1)} custom-call(s32[4]{0:T(128)S(1)} %copy-done.1, bf16[4,4,2,256,128]{4,3,2,1,0:T(8,128)(2,1)S(1)} %gather.1.pages_in, bf16[16,8192]{1,0:T(8,128)(2,1)S(1)} %collective-permute-done.3.queries, bf16[16,8192]{1,0:T(8,128)(2,1)S(1)} %attend_00.1.refs_0_), custom_call_target="tpu_custom_call" | custom-call | flops 6000000000 | bytes 4194304 | tf_op jit(solution)/shard_map/attend_01/pallas_call | solution.py:212
  33.6 1.3 %collective-permute-start.6 = (bf16[16,8192]{1,0:T(8,128)(2,1)S(1)}, bf16[16,8192]{1,0:T(8,128)(2,1)S(1)}, u32[]{:S(2)}, u32[]{:S(2)}) collective-permute-start(bf16[16,8192]{1,0:T(8,128)(2,1)S(1)} %attend_01.1), channel_id=1, source_target_pairs={{8,1},{10,3},{9,5},{11,7},{13,9},{15,11},{12,13},{14,15},{24,17},{... | collective-permute-start | bytes 786440 | tf_op jit(solution)/shard_map/ppermute | solution.py:163
  34.9 6.8 %collective-permute-done.9.refs_1_ = bf16[16,8192]{1,0:T(8,128)(2,1)S(1)} collective-permute-done((bf16[16,8192]{1,0:T(8,128)(2,1)S(1)}, bf16[16,8192]{1,0:T(8,128)(2,1)S(1)}, u32[]{:S(2)}, u32[]{:S(2)}) %collective-permute-start.9) | collective-permute-done | bytes 262176 | tf_op jit(solution)/shard_map/ppermute | solution.py:163
  41.7 0.0 collective-permute-done.8.refs_0_
  41.7 0.7 %join.3.refs_1_ = bf16[16,16384]{1,0:T(8,128)(2,1)} custom-call(bf16[16,8192]{1,0:T(8,128)(2,1)S(1)} %collective-permute-done.8.refs_0_, bf16[16,8192]{1,0:T(8,128)(2,1)S(1)} %collective-permute-done.9.refs_1_), custom_call_target="tpu_custom_call" | custom-call | tf_op jit(solution)/shard_map/join/pallas_call | solution.py:227
  42.4 0.0 collective-permute-done.7.refs_0_
  42.5 6.8 %collective-permute-done.6.refs_0_ = bf16[16,8192]{1,0:T(8,128)(2,1)S(1)} collective-permute-done((bf16[16,8192]{1,0:T(8,128)(2,1)S(1)}, bf16[16,8192]{1,0:T(8,128)(2,1)S(1)}, u32[]{:S(2)}, u32[]{:S(2)}) %collective-permute-start.6) | collective-permute-done | bytes 262176 | tf_op jit(solution)/shard_map/ppermute | solution.py:163
  49.3 0.7 %join.5 = bf16[16,16384]{1,0:T(8,128)(2,1)} custom-call(bf16[16,8192]{1,0:T(8,128)(2,1)S(1)} %collective-permute-done.6.refs_0_, bf16[16,16384]{1,0:T(8,128)(2,1)} %join.4.refs_1_), custom_call_target="tpu_custom_call", output_to_operand_aliasing={{}: (1, {})} | custom-call | tf_op jit(solution)/shard_map/join/pallas_call | solution.py:227
  (2 shorter events, 0.0 us)
Async XLA Ops:
  0.0 27.8 %collective-permute-start = (bf16[2,512,512]{2,1,0:T(8,128)(2,1)}, bf16[2,512,512]{2,1,0:T(8,128)(2,1)S(1)}, u32[]{:S(2)}, u32[]{:S(2)}) collective-permute-start(bf16[2,512,512]{2,1,0:T(8,128)(2,1)} %own.1), channel_id=1, source_target_pairs={{9,13},{11,15},{12,9},{14,11},{25,29},{27,31},{28,25},{30,27}} | collective-permute-start | bytes 3145736 | tf_op jit(solution)/shard_map/ppermute | solution.py:163
  1.8 11.1 %collective-permute-start.2 = (bf16[16,8192]{1,0:T(8,128)(2,1)S(1)}, bf16[16,8192]{1,0:T(8,128)(2,1)S(1)}, u32[]{:S(2)}, u32[]{:S(2)}) collective-permute-start(bf16[16,8192]{1,0:T(8,128)(2,1)S(1)} %get-tuple-element.7), channel_id=1, source_target_pairs={{0,10},{2,8},{4,11},{6,9},{8,15},{10,13},{12,14},{14,12},{16,26},{... | collective-permute-start | bytes 786440 | tf_op jit(solution)/shard_map/ppermute | solution.py:163
  2.5 25.4 %collective-permute-start.1 = (bf16[2,512,512]{2,1,0:T(8,128)(2,1)}, bf16[2,512,512]{2,1,0:T(8,128)(2,1)S(1)}, u32[]{:S(2)}, u32[]{:S(2)}) collective-permute-start(bf16[2,512,512]{2,1,0:T(8,128)(2,1)} %own.1), channel_id=1, source_target_pairs={{8,9},{9,8},{10,11},{11,10},{12,13},{13,12},{14,15},{15,14},{24,25... | collective-permute-start | bytes 3145736 | tf_op jit(solution)/shard_map/ppermute | solution.py:163
  3.2 26.5 %collective-permute-start.5 = (bf16[16,8192]{1,0:T(8,128)(2,1)S(1)}, bf16[16,8192]{1,0:T(8,128)(2,1)S(1)}, u32[]{:S(2)}, u32[]{:S(2)}) collective-permute-start(bf16[16,8192]{1,0:T(8,128)(2,1)S(1)} %get-tuple-element.7), channel_id=1, source_target_pairs={{1,10},{3,8},{5,11},{7,9},{9,15},{11,13},{13,14},{15,12},{17,26},{... | collective-permute-start | bytes 786440 | tf_op jit(solution)/shard_map/ppermute | solution.py:163
  12.0 15.8 %copy-start = (bf16[2,512,512]{2,1,0:T(8,128)(2,1)S(1)}, bf16[2,512,512]{2,1,0:T(8,128)(2,1)}, u32[]{:S(2)}) copy-start(bf16[2,512,512]{2,1,0:T(8,128)(2,1)} %own.1) | copy-start | bytes 3145732
  12.0 15.8 %copy-start.1 = (s32[4]{0:T(128)S(1)}, s32[4]{0:T(128)}, u32[]{:S(2)}) copy-start(s32[4]{0:T(128)} %counts.9) | copy-start | bytes 52
  12.0 19.5 %collective-permute-start.4 = (bf16[16,8192]{1,0:T(8,128)(2,1)S(1)}, bf16[16,8192]{1,0:T(8,128)(2,1)S(1)}, u32[]{:S(2)}, u32[]{:S(2)}) collective-permute-start(bf16[16,8192]{1,0:T(8,128)(2,1)S(1)} %get-tuple-element.8), channel_id=1, source_target_pairs={{0,8},{2,10},{4,9},{6,11},{8,13},{10,15},{12,12},{14,14},{16,24},{... | collective-permute-start | bytes 786440 | tf_op jit(solution)/shard_map/ppermute | solution.py:163
  12.9 20.0 %collective-permute-start.3 = (bf16[16,8192]{1,0:T(8,128)(2,1)S(1)}, bf16[16,8192]{1,0:T(8,128)(2,1)S(1)}, u32[]{:S(2)}, u32[]{:S(2)}) collective-permute-start(bf16[16,8192]{1,0:T(8,128)(2,1)S(1)} %get-tuple-element.8), channel_id=1, source_target_pairs={{1,8},{3,10},{5,9},{7,11},{9,13},{11,15},{13,12},{15,14},{17,24},{... | collective-permute-start | bytes 786440 | tf_op jit(solution)/shard_map/ppermute | solution.py:163
  29.0 12.7 %collective-permute-start.8 = (bf16[16,8192]{1,0:T(8,128)(2,1)S(1)}, bf16[16,8192]{1,0:T(8,128)(2,1)S(1)}, u32[]{:S(2)}, u32[]{:S(2)}) collective-permute-start(bf16[16,8192]{1,0:T(8,128)(2,1)S(1)} %attend_10.1.refs_0_), channel_id=1, source_target_pairs={{10,0},{8,2},{11,4},{9,6},{15,8},{13,10},{14,12},{12,14},{26,16},{... | collective-permute-start | bytes 786440 | tf_op jit(solution)/shard_map/ppermute | solution.py:163
  30.3 11.5 %collective-permute-start.9 = (bf16[16,8192]{1,0:T(8,128)(2,1)S(1)}, bf16[16,8192]{1,0:T(8,128)(2,1)S(1)}, u32[]{:S(2)}, u32[]{:S(2)}) collective-permute-start(bf16[16,8192]{1,0:T(8,128)(2,1)S(1)} %attend_11.1.refs_0_), channel_id=1, source_target_pairs={{10,1},{8,3},{11,5},{9,7},{15,9},{13,11},{14,13},{12,15},{26,17},{... | collective-permute-start | bytes 786440 | tf_op jit(solution)/shard_map/ppermute | solution.py:163
  32.1 10.3 %collective-permute-start.7 = (bf16[16,8192]{1,0:T(8,128)(2,1)S(1)}, bf16[16,8192]{1,0:T(8,128)(2,1)S(1)}, u32[]{:S(2)}, u32[]{:S(2)}) collective-permute-start(bf16[16,8192]{1,0:T(8,128)(2,1)S(1)} %attend_00.1.refs_0_), channel_id=1, source_target_pairs={{8,0},{10,2},{9,4},{11,6},{13,8},{15,10},{12,12},{14,14},{24,16},{... | collective-permute-start | bytes 786440 | tf_op jit(solution)/shard_map/ppermute | solution.py:163
  33.6 15.7 %collective-permute-start.6 = (bf16[16,8192]{1,0:T(8,128)(2,1)S(1)}, bf16[16,8192]{1,0:T(8,128)(2,1)S(1)}, u32[]{:S(2)}, u32[]{:S(2)}) collective-permute-start(bf16[16,8192]{1,0:T(8,128)(2,1)S(1)} %attend_01.1), channel_id=1, source_target_pairs={{8,1},{10,3},{9,5},{11,7},{13,9},{15,11},{12,13},{14,15},{24,17},{... | collective-permute-start | bytes 786440 | tf_op jit(solution)/shard_map/ppermute | solution.py:163
